TPU v7x, 128 devices: a whole 4x4x4 slice. The times are simulated.
128 devices in a mesh: block: 16 (over z_hi, x, core), tm: 8 (over y, z_lo).
Axes of the slice: x: 4, y: 4, z: 4 (z_hi: 2, z_lo: 2; z = z_hi * 2 + z_lo), core: 2. Of those that a mesh axis runs over, the one named last changes fastest.
Arguments:
- traces: bfloat16 [4096, 16, 6, 1024], P('block', 'tm')
- valid: int32 [4096, 16, 6], P('block', 'tm'), may hold values from 0 to 1, as said below
- panel_owner: int32 [4], replicated, may hold values from 0 to 15, as said below
- panel_start: int32 [4], replicated, may hold values from 0 to 252, as said below
Outputs:
- xcorr: float32 [16, 4096, 1024], P('tm', 'block')
Inputs may be any that keep to these rules, and one draw needn't show every extreme that they name: Within one block-tm cell (256 channels by 2 windows by 6 segments) at least an eighth of the segments are valid. `panel_owner`: the panels lie on distinct blocks. `panel_start`: multiples of 4.
All inputs are finite; a program needn't handle non-finite values.
Results may differ from a plain program's by a relative error of at most 0.0051.
Values may be sent and summed in bfloat16 or wider, within the bound.
A program may use at most 128 MiB of HBM per device.

v0:
```python
import math

import jax
import jax.numpy as jnp
from jax import lax
from jax.sharding import PartitionSpec as P

PP = 4
NP = 4


def spread(value, axis, source):
    kept = jnp.where(lax.axis_index(axis) == source, value, 0).astype(value.dtype)
    return lax.psum(kept, axis)


def forward_table(length):
    sample = jnp.arange(length, dtype=jnp.int32)
    bin_index = jnp.arange(length // 2, dtype=jnp.int32)
    angles = (sample[:, None] * bin_index[None, :] % length).astype(jnp.float32) * (
        2.0 * math.pi / length
    )
    return jnp.concatenate([jnp.cos(angles), -jnp.sin(angles)], axis=1).astype(jnp.bfloat16)


def inverse_table(length, factor):
    bin_index = jnp.arange(length // 2, dtype=jnp.int32)
    lag_index = jnp.arange(length, dtype=jnp.int32)
    angles = (bin_index[:, None] * lag_index[None, :] % length).astype(jnp.float32) * (
        2.0 * math.pi / length
    )
    weight = jnp.where(bin_index == 0, 1.0, 2.0).astype(jnp.float32)[:, None] * factor
    return jnp.concatenate([weight * jnp.cos(angles), -weight * jnp.sin(angles)], axis=0)


def whiten(segment_rows, valid_mask, forward):
    spectrum = jnp.dot(segment_rows, forward, preferred_element_type=jnp.float32)
    energy = jnp.mean(spectrum * spectrum, axis=1, keepdims=True)
    return (spectrum * lax.rsqrt(energy + 1e-06) * valid_mask[:, None].astype(jnp.float32)).astype(
        jnp.bfloat16
    )


def spectra_rows(segment_rows, valid_mask, forward):
    return whiten(segment_rows, valid_mask, forward)


def correlate(left, right):
    bins = left.shape[-1] // 2
    left_both = jnp.concatenate([left[..., :bins], left[..., bins:]], axis=1)
    right_both = jnp.concatenate([right[..., :bins], right[..., bins:]], axis=1)
    right_turn = jnp.concatenate([right[..., bins:], -right[..., :bins]], axis=1)
    real_part = jnp.einsum(
        "jmk,imk->jik", left_both, right_both, preferred_element_type=jnp.float32
    )
    imag_part = jnp.einsum(
        "jmk,imk->jik", left_both, right_turn, preferred_element_type=jnp.float32
    )
    return jnp.concatenate([real_part, imag_part], axis=-1)


def fetch_panel(whitened, panel_root, panel_first):
    candidate = lax.dynamic_slice_in_dim(whitened, panel_first, PP, 0)
    return spread(candidate, "block", panel_root)


def on_device(traces, valid, panel_owner, panel_start):
    channels, windows_here, segments, length = traces.shape
    bins = length // 2
    forward = forward_table(length)
    whitened = spectra_rows(
        traces.reshape(channels * windows_here * segments, length),
        valid.reshape(channels * windows_here * segments),
        forward,
    )
    whitened = whitened.reshape(channels, windows_here, segments, 2 * bins)
    pieces = []
    for panel in range(NP):
        pieces.append(fetch_panel(whitened, panel_owner[panel], panel_start[panel]))
    sources = jnp.concatenate(pieces, axis=0)
    groups = lax.axis_size("tm")
    inverse = inverse_table(length, 1.0 / math.sqrt(bins * windows_here * segments * groups))
    source_count = sources.shape[0]
    own_rows = whitened.reshape(channels, windows_here * segments, 2 * bins)
    source_rows = sources.reshape(source_count, windows_here * segments, 2 * bins)
    stacked = lax.psum_scatter(
        correlate(source_rows, own_rows), "tm", scatter_dimension=0, tiled=True
    )
    return jnp.dot(stacked, inverse, precision=lax.Precision.HIGHEST)


def solution(mesh):
    in_specs = (P("block", "tm", None, None), P("block", "tm", None), P(), P())
    out_specs = P("tm", "block", None)
    return jax.shard_map(
        on_device, mesh=mesh, in_specs=in_specs, out_specs=out_specs, check_vma=False
    )
```

profile of v0, /device:TPU:0, one launch (start us, length us, event | category | flops | bytes accessed | tf_op | source)
XLA Modules:
  0.0 627.8 jit_solution(12414419211468967109)
XLA Ops:
  6.5 0.0 all-reduce.3.cloned.1.call-start
  6.5 1.5 fusion.26
  13.2 8.5 %negate_convert_fusion = (bf16[1024,512]{1,0:T(8,128)(2,1)S(1)}, bf16[1024,512]{1,0:T(8,128)(2,1)S(1)}) fusion(), kind=kLoop, calls=%fused_computation.30 | loop fusion | flops 8912896 | bytes 2097152 | tf_op jit(solution)/shard_map/convert.1
  21.7 8.9 %copy.5 = bf16[256,2,6,1024]{3,2,1,0:T(8,128)(2,1)} copy(bf16[256,2,6,1024]{3,1,2,0:T(2,128)(2,1)} %param.4) | data formatting | bytes 12582912 | tf_op args[0]
  30.7 11.0 %reshape.36 = bf16[3072,1024]{1,0:T(8,128)(2,1)} reshape(bf16[256,2,6,1024]{3,2,1,0:T(8,128)(2,1)} %copy.5) | data formatting | bytes 12582912 | tf_op jit(solution)/shard_map/reshape | solution.py:72
  41.7 0.0 copy-start
  41.7 12.5 %multiply_reduce_fusion = (f32[3072]{0:T(1024)S(1)}, f32[1024,3072]{1,0:T(8,128)}) fusion(bf16[3072,1024]{1,0:T(8,128)(2,1)} %reshape.36, bf16[1024,512]{1,0:T(8,128)(2,1)S(1)} %get-tuple-element.30, bf16[1024,512]{1,0:T(8,128)(2,1)S(1)} %get-tuple-element.31), kind=kOutput, calls=%fused_computation.2 | convolution fusion | flops 6452933632 | bytes 20983808 | tf_op jit(solution)/shard_map/dot_general | solution.py:37
  54.2 0.0 copy-done
  54.2 0.2 copy.6
  54.4 0.3 convert_element_type.35
  54.7 9.0 %fusion = bf16[3072,1024]{0,1:T(8,128)(2,1)} fusion(f32[1024,3072]{1,0:T(8,128)} %get-tuple-element.29, f32[3072]{0:T(1024)S(1)} %convert_element_type.35, f32[3072]{0:T(1024)S(1)} %add_rsqrt_fusion), kind=kLoop, calls=%fused_computation.3 | loop fusion | flops 9437184 | bytes 18898944 | tf_op jit(solution)/shard_map/convert_element_type | solution.py:39
  63.7 8.6 %copy.7 = bf16[3072,1024]{1,0:T(8,128)(2,1)} copy(bf16[3072,1024]{0,1:T(8,128)(2,1)} %fusion) | data formatting | bytes 12582912 | tf_op jit(solution)/shard_map/convert_element_type | solution.py:39
  72.3 0.0 copy-start.1
  72.3 11.0 %reshape.37 = bf16[256,2,6,1024]{3,2,1,0:T(8,128)(2,1)} reshape(bf16[3072,1024]{1,0:T(8,128)(2,1)} %copy.7) | data formatting | bytes 12582912 | tf_op jit(solution)/shard_map/reshape | solution.py:76
  83.3 0.0 copy-done.1
  83.3 0.7 fusion.25
  89.0 1.9 dynamic-slice_select_fusion.3
  90.9 0.0 all-reduce.3.cloned.1.call-update
  91.0 0.2 reduce-scatter.2.cloned.1.call-start
  91.2 10.6 %reshape_reshape.3 = bf16[256,12,1024]{2,1,0:T(8,128)(2,1)} reshape(bf16[3072,1024]{1,0:T(8,128)(2,1)} %copy.7) | data formatting | bytes 12582912 | tf_op jit(solution)/shard_map/reshape;reshape | solution.py:84
  101.8 3.9 fusion.23
  105.7 7.7 %pad_maximum_fusion.1 = (bf16[256,24,512]{2,1,0:T(8,128)(2,1)}, bf16[256,24,512]{2,1,0:T(8,128)(2,1)}) fusion(bf16[256,12,512]{2,1,0:T(8,128)(2,1)S(1)} %get-tuple-element.11, bf16[256,12,512]{2,1,0:T(8,128)(2,1)S(1)} %get-tuple-element.9, bf16[256,12,512]{2,1,0:T(8,128)(2,1)S(1)} %get-tuple-element.10), kind=kLoop, calls=%fused_computation.4 | loop fusion | flops 25165824 | bytes 22020096 | tf_op jit(solution)/shard_map/concatenate | solution.py:51
  113.5 9.6 %copy.10 = bf16[256,24,512]{0,1,2:T(8,128)(2,1)} copy(bf16[256,24,512]{2,1,0:T(8,128)(2,1)} %get-tuple-element.16) | data formatting | bytes 12582912 | tf_op jit(solution)/shard_map/concatenate | solution.py:51
  123.1 9.6 %copy.13 = bf16[256,24,512]{0,1,2:T(8,128)(2,1)} copy(bf16[256,24,512]{2,1,0:T(8,128)(2,1)} %get-tuple-element.17) | data formatting | bytes 12582912 | tf_op jit(solution)/shard_map/concatenate | solution.py:52
  132.6 100.0 %all-reduce.3.cloned.1.call-done = (bf16[4,2,6,1024]{3,2,1,0:T(8,128)(2,1)}, bf16[4,2,6,1024]{3,2,1,0:T(8,128)(2,1)}, bf16[4,2,6,1024]{3,2,1,0:T(8,128)(2,1)}, bf16[4,2,6,1024]{3,2,1,0:T(8,128)(2,1)}) async-done(((bf16[4,2,6,1024]{3,2,1,0:T(8,128)(2,1)}, bf16[4,2,6,1024]{3,2,1,0:T(8,128)(2,1)}, bf16[4,2,6,1024]{3,2,1,0:T(8,128)(2,1)}, bf16[4,2,6,1024]{3,2,1,0:T(8,128)(2,1)}), ...) | async-done | bytes 393232 | tf_op jit(solution)/shard_map/psum | solution.py:14
  232.6 1.2 pad_maximum_fusion.3
  233.9 0.2 copy.9
  234.2 2.1 copy.11
  236.3 7.2 %fusion.27 = f32[512,256,16]{1,2,0:T(8,128)} fusion(bf16[256,24,512]{0,1,2:T(8,128)(2,1)} %copy.10, bf16[16,24,512]{1,0,2:T(8,128)(2,1)S(1)} %copy.11), kind=kOutput, calls=%fused_computation.53 | convolution fusion | flops 100663296 | bytes 15073280 | tf_op jit(solution)/shard_map/jmk,imk->jik/dot_general | solution.py:53
  243.6 10.0 %copy.12 = f32[512,256,16]{0,1,2:T(8,128)} copy(f32[512,256,16]{1,2,0:T(8,128)} %fusion.27) | data formatting | bytes 16777216 | tf_op jit(solution)/shard_map/jmk,imk->jik/dot_general | solution.py:53
  253.5 7.2 %fusion.28 = f32[512,256,16]{1,2,0:T(8,128)} fusion(bf16[256,24,512]{0,1,2:T(8,128)(2,1)} %copy.13, bf16[16,24,512]{1,0,2:T(8,128)(2,1)S(1)} %copy.11), kind=kOutput, calls=%fused_computation.54 | convolution fusion | flops 100663296 | bytes 15073280 | tf_op jit(solution)/shard_map/jmk,imk->jik/dot_general | solution.py:56
  260.8 10.0 %copy.14 = f32[512,256,16]{0,1,2:T(8,128)} copy(f32[512,256,16]{1,2,0:T(8,128)} %fusion.28) | data formatting | bytes 16777216 | tf_op jit(solution)/shard_map/jmk,imk->jik/dot_general | solution.py:56
  270.7 11.8 %pad_maximum_fusion = f32[16,256,1024]{2,1,0:T(8,128)} fusion(f32[16,256,512]{2,1,0:T(8,128)} %bitcast.23, f32[16,256,512]{2,1,0:T(8,128)} %bitcast.22), kind=kLoop, calls=%fused_computation | loop fusion | flops 4194304 | bytes 33554432 | tf_op jit(solution)/shard_map/concatenate | solution.py:59
  282.5 0.0 reduce-scatter.2.cloned.1.call-update
  282.5 9.2 %sine_multiply_fusion = (f32[512,1024]{1,0:T(8,128)S(1)}, f32[512,1024]{1,0:T(8,128)}) fusion(f32[512]{0:T(512)S(1)} %fusion.20, f32[512]{0:T(512)S(1)} %select_multiply_fusion), kind=kLoop, calls=%fused_computation.26 | loop fusion | flops 8388608 | bytes 4198400 | tf_op jit(solution)/shard_map/mul | solution.py:33
  291.7 318.3 %reduce-scatter.2.cloned.1.call-done = f32[2,256,1024]{2,1,0:T(8,128)} async-done(((f32[16,256,1024]{2,1,0:T(8,128)}), f32[2,256,1024]{2,1,0:T(8,128)}) %reduce-scatter.2.cloned.1.call-update) | async-done | bytes 2097168 | tf_op jit(solution)/shard_map/reduce_scatter | solution.py:86
  610.0 11.0 %fusion.1 = f32[2,256,1024]{2,1,0:T(8,128)} fusion(f32[2,256,1024]{2,1,0:T(8,128)} %reduce-scatter.2.cloned.1.call-done, f32[512,1024]{1,0:T(8,128)S(1)} %get-tuple-element.32, f32[512,1024]{1,0:T(8,128)} %get-tuple-element.33), kind=kOutput, calls=%fused_computation.7 | convolution fusion | flops 6443499520 | bytes 8388608 | tf_op jit(solution)/shard_map/dot_general | solution.py:89
  (6 shorter events, 0.1 us)
Async XLA Ops:
  6.5 226.1 %all-reduce.3.cloned.1.call-start = ((), (), s32[]{:S(2)}) async-start(), calls=%async_computation.2 | async-start | bytes 1048576 | tf_op jit(solution)/shard_map/psum | solution.py:14
  41.7 12.5 %copy-start = (s32[256,2,6]{0,1,2:T(2,128)S(1)}, s32[256,2,6]{0,1,2:T(2,128)}, u32[]{:S(2)}) copy-start(s32[256,2,6]{0,1,2:T(2,128)} %param.5) | copy-start | bytes 36868
  72.3 11.0 %copy-start.1 = (s32[4]{0:T(128)S(1)}, s32[4]{0:T(128)}, u32[]{:S(2)}) copy-start(s32[4]{0:T(128)} %param.6) | copy-start | bytes 52
  91.0 519.1 %reduce-scatter.2.cloned.1.call-start = ((), (), s32[]{:S(2)}) async-start(), calls=%async_computation.1 | async-start | bytes 18874368 | tf_op jit(solution)/shard_map/reduce_scatter | solution.py:86
Sparse Core Ops, SparseCore 0:
  91.1 141.5 all-reduce.2
  282.6 327.3 reduce-scatter.1
where the time goes:
time: 631 us; the launch traced here: 628 us
  waiting for transfers between devices  418 us (66%)
  local copies, waits for them, and re-layouts  94.3 us (15%)
  other arithmetic  53.3 us (8%)
  matrix products  37.9 us (6%)
  between operations  23.7 us (4%)
    reduce_scatter x1, waiting for transfers between devices, on_device(): lax.psum_scatter(correlate(source_rows, own_rows), 'tm', scatter_dimensio...  318 us
    psum x1, waiting for transfers between devices, spread(): return lax.psum(kept, axis)  100 us
  transfers between devices with their start and end apart: 2, of which 2 were waited for; matrix products, arithmetic and copies ran while one was open for 8% of the time, Pallas kernels for 0%

commit v1 on v0

v1 whole, which is shorter than its diff:
```python
import functools
import math

import jax
import jax.numpy as jnp
import ml_dtypes
import numpy as np
from jax import lax
from jax.experimental import pallas as pl
from jax.experimental.pallas import tpu as pltpu
from jax.sharding import PartitionSpec as P

MESH = pl.DeviceIdType.MESH
PP = 4
NP = 4
J = PP * NP
GB = 8
PAIR = 2 * GB
KB = 32
GP = KB // PAIR
RJ = GP * 2 * PAIR
NZ = 8
NT = (((1,), (1,)), ((), ()))


def forward_t(length):
    k = np.arange(length // 2)
    n = np.arange(length)
    a = (k[:, None] * n[None, :] % length) * (2.0 * math.pi / length)
    return np.concatenate([np.cos(a), -np.sin(a)], axis=0).astype(np.float32).astype(ml_dtypes.bfloat16)


def inverse_rows(length, factor):
    bins = length // 2
    k = np.arange(bins)
    t = np.arange(length)
    a = (k[:, None] * t[None, :] % length) * (2.0 * math.pi / length)
    w = np.where(k == 0, 1.0, 2.0)[:, None] * factor
    full = np.stack([w * np.cos(a), -w * np.sin(a)])
    full = full.reshape(2, bins // PAIR, PAIR, length).transpose(1, 0, 2, 3)
    return full.reshape(length, length).astype(np.float32).astype(ml_dtypes.bfloat16)


def kernel(dims, x_hbm, ft_hbm, slab, onehot, valid, c_out, xv, ftv, w, scale, p, s, xs,
           rsb, rz1, zfl, zfr, zrl, zrr, yfl, yfr, yrl, yrr, zs, rz2,
           x_sem, ft_sem, rs_send, rs_recv, own_sem, ag_send, ag_recv,
           z1_send, z1_recv, zy_send, zfl_recv, zfr_recv, zrl_recv, zrr_recv,
           yy_send, yfl_recv, yfr_recv, yrl_recv, yrr_recv, z2_send, z2_recv):
    nb, nt, m_count, length = dims
    bins = length // 2
    channels = c_out.shape[-1]
    ny = nt // 2
    nr = nb // 2
    b = lax.axis_index("block")
    t = lax.axis_index("tm")
    y = t // 2
    z = t % 2
    right = (b, (y + 1) % ny * 2 + z)
    left = (b, (y + ny - 1) % ny * 2 + z)
    across = (b, y * 2 + 1 - z)
    yr = (y + 1) % ny
    yl = (y + ny - 1) % ny
    yo = (y + 2) % ny

    def remote(src, dst, send, recv, device):
        return pltpu.make_async_remote_copy(
            src_ref=src, dst_ref=dst, send_sem=send, recv_sem=recv,
            device_id=device, device_id_type=MESH,
        )

    pltpu.make_async_copy(ft_hbm, ftv, ft_sem).start()

    def load(m):
        return pltpu.make_async_copy(x_hbm.at[m], xv.at[m], x_sem.at[m])

    def start_load(m, _):
        load(m).start()
        return 0

    lax.fori_loop(0, m_count, start_load, 0)

    barrier = pltpu.get_barrier_semaphore()

    def greet(e, _):
        @pl.when(e != b)
        def _():
            pl.semaphore_signal(barrier, inc=1, device_id=(e, t), device_id_type=MESH)

        return 0

    lax.fori_loop(0, nb, greet, 0)
    for device in (right, left, across):
        pl.semaphore_signal(barrier, inc=1, device_id=device, device_id_type=MESH)
    pl.semaphore_wait(barrier, nb - 1 + 3)

    def rs_copy(r):
        return remote(slab.at[r], rsb.at[b], rs_send.at[r], rs_recv.at[b], (2 * r, t))

    def rs_start(r, _):
        @pl.when(2 * r != b)
        def _():
            rs_copy(r).start()

        return 0

    lax.fori_loop(0, nr, rs_start, 0)
    reducer = b % 2 == 0
    part = b // 2

    @pl.when(reducer)
    def _():
        pltpu.make_async_copy(slab.at[part], rsb.at[b], own_sem).start()

    def transform(m):
        load(m).wait()
        spectrum = lax.dot_general(ftv[...], xv[m], NT, preferred_element_type=jnp.float32)
        w[m] = spectrum
        energy = jnp.sum(spectrum * spectrum, axis=0, keepdims=True) * (1.0 / length)
        scale[m] = lax.rsqrt(energy + 1e-06) * valid[m]

    def transform_step(m, _):
        transform(m)
        return 0

    pltpu.make_async_copy(ft_hbm, ftv, ft_sem).wait()
    early = m_count // 3
    lax.fori_loop(0, early, transform_step, 0)

    rows_s = m_count * J

    def ag_copy(e):
        return remote(
            xs.at[part], xs.at[part], ag_send.at[e], ag_recv.at[part], (e, t)
        )

    @pl.when(reducer)
    def _():
        pltpu.make_async_copy(slab.at[part], rsb.at[b], own_sem).wait()

        def rs_wait(e, _):
            @pl.when(e != b)
            def _():
                remote(slab.at[0], rsb.at[e], rs_send.at[0], rs_recv.at[e], (e, t)).wait_recv()

            return 0

        lax.fori_loop(0, nb, rs_wait, 0)
        picked = jnp.dot(
            onehot[...], rsb[...].reshape(nb * m_count * PP, length // nr),
            preferred_element_type=jnp.float32,
        )
        xs[part] = picked.astype(jnp.bfloat16)

        def ag_start(e, _):
            @pl.when(e != b)
            def _():
                ag_copy(e).start()

            return 0

        lax.fori_loop(0, nb, ag_start, 0)

    lax.fori_loop(early, m_count, transform_step, 0)

    def ag_wait(r, _):
        @pl.when(2 * r != b)
        def _():
            remote(xs.at[r], xs.at[r], ag_send.at[0], ag_recv.at[r], (2 * r, t)).wait_recv()

        return 0

    lax.fori_loop(0, nr, ag_wait, 0)
    source_rows = jnp.concatenate([xs[r] for r in range(nr)], axis=1)
    source_rows = jnp.concatenate(
        [source_rows, jnp.zeros((256 - rows_s, length), jnp.bfloat16)], axis=0
    )
    spectrum = lax.dot_general(ftv[...], source_rows, NT, preferred_element_type=jnp.float32)
    energy = jnp.sum(spectrum * spectrum, axis=0, keepdims=True) * (1.0 / length)
    s[...] = spectrum * lax.rsqrt(energy + 1e-06)

    def iota(shape, axis):
        return lax.broadcasted_iota(jnp.int32, shape, axis)

    def correlate_group(k0):
        copies = (iota((128, 256), 0) // GB == iota((128, 256), 1) % J).astype(jnp.float32)
        copies = copies.astype(jnp.bfloat16)
        segment = iota((128, 256), 0) // GB == iota((128, 256), 1) // J
        diagonal = iota((128, 256), 0) % GB == iota((128, 256), 1) % GB
        stacked = []
        for base in (0, bins):
            tile = s[pl.ds(pl.multiple_of(base + k0, GB), GB), :]
            stacked.append(jnp.where(segment, jnp.concatenate([tile] * 16, axis=0), 0.0))
        stacked = jnp.concatenate(stacked, axis=0).astype(jnp.bfloat16)
        real = lax.dot_general(copies, stacked, NT, preferred_element_type=jnp.float32)
        real = jnp.where(diagonal, real, 0.0)
        imag = jnp.concatenate([-real[:, 128:], real[:, :128]], axis=1)
        left_side = jnp.concatenate([real, imag], axis=0).astype(jnp.bfloat16)
        rows = []
        for base in (0, bins):
            for m in range(m_count):
                tile = w[m, pl.ds(pl.multiple_of(base + k0, GB), GB), :]
                rows.append(tile * scale[m])
            rows.append(jnp.zeros((128 - m_count * GB, channels), jnp.float32))
        right_side = jnp.concatenate(rows, axis=0).astype(jnp.bfloat16)
        return jnp.dot(left_side, right_side, preferred_element_type=jnp.float32)

    def correlate_chunk(c):
        for g in range(GP):
            k0 = c * KB + g * PAIR
            first = correlate_group(k0).reshape(2, J, GB, channels)
            second = correlate_group(k0 + GB).reshape(2, J, GB, channels)
            both = jnp.concatenate([first, second], axis=2).astype(jnp.bfloat16)
            both = both.reshape(2, ny, 2, 2, PAIR, channels)
            for o in range(2):
                p[c, :, :, :, pl.ds((g * 2 + o) * PAIR, PAIR), :] = both[o]

    def z1(n):
        return remote(p.at[n, :, 1 - z], rz1.at[n], z1_send.at[n], z1_recv.at[n], across)

    def ring(parts, n, fl, fr, rl, rr, send, fl_recv, fr_recv, rl_recv, rr_recv):
        def copy(i):
            src, dst, recv, device = (
                lambda: (parts(yo, 0), fl.at[n], fl_recv.at[n], right),
                lambda: (parts(yo, 1), fr.at[n], fr_recv.at[n], left),
                lambda: (parts(yr, 1), rl.at[n, 1], rl_recv.at[n, 1], right),
                lambda: (parts(yl, 0), rr.at[n, 0], rr_recv.at[n, 0], left),
                lambda: (fl.at[n], rl.at[n, 0], rl_recv.at[n, 0], right),
                lambda: (fr.at[n], rr.at[n, 1], rr_recv.at[n, 1], left),
            )[i]()
            return remote(src, dst, send.at[n, i], recv, device)

        return copy

    def add(a, c):
        return (a.astype(jnp.float32) + c.astype(jnp.float32)).astype(jnp.bfloat16)

    def z_ring(n):
        return ring(lambda o, h: rz1.at[n, o, h], n, zfl, zfr, zrl, zrr,
                    zy_send, zfl_recv, zfr_recv, zrl_recv, zrr_recv)

    def y_ring(n):
        return ring(lambda o, h: p.at[NZ + n, o, h], n, yfl, yfr, yrl, yrr,
                    yy_send, yfl_recv, yfr_recv, yrl_recv, yrr_recv)

    def z2(n):
        return remote(zs.at[n], rz2.at[n], z2_send.at[n], z2_recv.at[n], across)

    def slot(n, _):
        @pl.when(n < NZ)
        def _():
            correlate_chunk(n)
            z1(n).start()
            correlate_chunk(NZ + n)
            for i in range(4):
                y_ring(n)(i).start()

        @pl.when((n >= 1) & (n < NZ + 1))
        def _():
            k = n - 1
            copies = y_ring(k)
            copies(0).wait_recv()
            yfl[k] = add(yfl[k], p[NZ + k, yr, 0])
            copies(4).start()
            copies(1).wait_recv()
            yfr[k] = add(yfr[k], p[NZ + k, yl, 1])
            copies(5).start()
            z1(k).wait_recv()
            rz1[k] = add(rz1[k], p[k, :, z])
            for i in range(4):
                z_ring(k)(i).start()

        @pl.when((n >= 2) & (n < NZ + 2))
        def _():
            k = n - 2
            copies = y_ring(k)
            for i in (2, 3, 4, 5):
                copies(i).wait_recv()
            total = (p[NZ + k, y].astype(jnp.float32) + yrl[k].astype(jnp.float32)
                     + yrr[k].astype(jnp.float32))
            zs[k] = jnp.where(z == 0, total[1], total[0]).astype(jnp.bfloat16)
            c_out[:, NZ + k] = jnp.where(z == 0, total[0], total[1])
            z2(k).start()
            copies = z_ring(k)
            copies(0).wait_recv()
            zfl[k] = add(zfl[k], rz1[k, yr, 0])
            copies(4).start()
            copies(1).wait_recv()
            zfr[k] = add(zfr[k], rz1[k, yl, 1])
            copies(5).start()

        @pl.when(n >= 3)
        def _():
            k = n - 3
            copies = z_ring(k)
            for i in (2, 3, 4, 5):
                copies(i).wait_recv()
            c_out[:, k] = (rz1[k, y].astype(jnp.float32) + zrl[k].astype(jnp.float32)
                           + zrr[k].astype(jnp.float32))
            z2(k).wait_recv()
            c_out[:, NZ + k] += rz2[k].astype(jnp.float32)

        return 0

    lax.fori_loop(0, NZ + 3, slot, 0)

    def rs_drain(r, _):
        @pl.when(2 * r != b)
        def _():
            rs_copy(r).wait_send()

        return 0

    lax.fori_loop(0, nr, rs_drain, 0)

    @pl.when(reducer)
    def _():
        def ag_drain(e, _):
            @pl.when(e != b)
            def _():
                ag_copy(e).wait_send()

            return 0

        lax.fori_loop(0, nb, ag_drain, 0)

    def drain(n, _):
        z1(n).wait_send()
        z2(n).wait_send()
        for i in range(6):
            z_ring(n)(i).wait_send()
            y_ring(n)(i).wait_send()
        return 0

    lax.fori_loop(0, NZ, drain, 0)


def on_device(traces, valid, panel_owner, panel_start):
    channels, windows_here, segments, length = traces.shape
    m_count = windows_here * segments
    nb = lax.axis_size("block")
    nt = lax.axis_size("tm")
    nr = nb // 2
    ny = nt // 2
    b = lax.axis_index("block")
    x = traces.transpose(1, 2, 0, 3).reshape(m_count, channels, length)
    mine = panel_owner == b
    start = jnp.sum(jnp.where(mine, panel_start, 0))
    slab = lax.dynamic_slice_in_dim(traces, start, PP, 0)
    slab_valid = lax.dynamic_slice_in_dim(valid, start, PP, 0)
    slab = jnp.where(slab_valid[..., None] != 0, slab, 0).astype(jnp.bfloat16)
    slab = slab.transpose(1, 2, 0, 3).reshape(m_count * PP, nr, length // nr).transpose(1, 0, 2)
    mask = valid.transpose(1, 2, 0).reshape(m_count, 1, channels).astype(jnp.float32)
    row = jnp.arange(m_count * J, dtype=jnp.int32)
    col = jnp.arange(nb * m_count * PP, dtype=jnp.int32)
    owner = jnp.tile(jnp.repeat(panel_owner, PP), m_count)
    onehot = (
        (owner[:, None] == (col // (m_count * PP))[None, :])
        & ((row // J)[:, None] == (col // PP % m_count)[None, :])
        & ((row % PP)[:, None] == (col % PP)[None, :])
    ).astype(jnp.bfloat16)
    forward = jnp.asarray(forward_t(length))
    inverse = jnp.asarray(
        inverse_rows(length, 1.0 / math.sqrt(length // 2 * m_count * nt))
    )
    bf16, f32 = jnp.bfloat16, jnp.float32
    dma = pltpu.SemaphoreType.DMA
    vmem = pl.BlockSpec(memory_space=pltpu.VMEM)
    hbm = pl.BlockSpec(memory_space=pl.ANY)
    chunks = 2 * NZ
    unit = (RJ, channels)
    cross = pl.pallas_call(
        functools.partial(kernel, (nb, nt, m_count, length)),
        out_shape=jax.ShapeDtypeStruct((2, chunks) + unit, f32),
        in_specs=[hbm, hbm, vmem, vmem, vmem],
        out_specs=vmem,
        scratch_shapes=[
            pltpu.VMEM((m_count, channels, length), bf16),
            pltpu.VMEM((length, length), bf16),
            pltpu.VMEM((m_count, length, channels), f32),
            pltpu.VMEM((m_count, 1, channels), f32),
            pltpu.VMEM((chunks, ny, 2, 2) + unit, bf16),
            pltpu.VMEM((length, 256), f32),
            pltpu.VMEM((nr, m_count * J, length // nr), bf16),
            pltpu.VMEM((nb, m_count * PP, length // nr), bf16),
            pltpu.VMEM((NZ, ny, 2) + unit, bf16),
            pltpu.VMEM((NZ,) + unit, bf16),
            pltpu.VMEM((NZ,) + unit, bf16),
            pltpu.VMEM((NZ, 2) + unit, bf16),
            pltpu.VMEM((NZ, 2) + unit, bf16),
            pltpu.VMEM((NZ, 2) + unit, bf16),
            pltpu.VMEM((NZ, 2) + unit, bf16),
            pltpu.VMEM((NZ, 2, 2) + unit, bf16),
            pltpu.VMEM((NZ, 2, 2) + unit, bf16),
            pltpu.VMEM((NZ, 2) + unit, bf16),
            pltpu.VMEM((NZ, 2) + unit, bf16),
            dma((m_count,)), dma, dma((nr,)), dma((nb,)), dma, dma((nb,)), dma((nr,)),
            dma((NZ,)), dma((NZ,)),
            dma((NZ, 6)), dma((NZ,)), dma((NZ,)), dma((NZ, 2)), dma((NZ, 2)),
            dma((NZ, 6)), dma((NZ,)), dma((NZ,)), dma((NZ, 2)), dma((NZ, 2)),
            dma((NZ,)), dma((NZ,)),
        ],
        compiler_params=pltpu.CompilerParams(
            collective_id=0, has_side_effects=True, vmem_limit_bytes=56 * 2**20
        ),
        name="cross",
    )(x, forward, slab, onehot, mask)
    cross = cross.reshape(2, length, channels).astype(bf16)
    return lax.dot_general(
        cross, inverse, (((1,), (0,)), ((), ())), preferred_element_type=f32
    )


def solution(mesh):
    in_specs = (P("block", "tm", None, None), P("block", "tm", None), P(), P())
    out_specs = P("tm", "block", None)
    return jax.shard_map(
        on_device, mesh=mesh, in_specs=in_specs, out_specs=out_specs, check_vma=False
    )
```

time: 631 us -> 109 us (0.17)
  waiting for transfers between devices: 418 us -> 0 us
  Pallas kernels: 0 us -> 87.1 us
  local copies, waits for them, and re-layouts: 94.3 us -> 11.2 us
  other arithmetic: 53.3 us -> 5.9 us
  matrix products: 37.9 us -> 2.59 us
  between operations: 23.7 us -> 2 us
    reduce_scatter x1 -> x0, waiting for transfers between devices: 318 us -> none  [on_device(): lax.psum_scatter(correlate(source_rows, own_rows), 'tm', scatter_dimensio...]
    psum x1 -> x0, waiting for transfers between devices: 100 us -> none  [spread(): return lax.psum(kept, axis)]
    pallas_call x0 -> x1, Pallas kernels: none -> 87.1 us  [on_device(): pl.pallas_call(functools.partial(kernel, (nb, nt, m_count, length)), out_...]
    dot_general x4 -> x1, matrix products: 37.9 us -> 2.59 us  [on_device(): lax.dot_general(cross, inverse, (((1,), (0,)), ((), ())), preferred_eleme...]
    concatenate x4 -> x0, local copies, waits for them, and re-layouts: 21.5 us -> none  [the longest x1 9.6 us: correlate(): right_both = jnp.concatenate([right[..., :bins], right[..., bins:]], axis=1)]
    reshape x2, local copies, waits for them, and re-layouts: 22 us -> 0.71 us  [on_device(): slab.transpose(1, 2, 0, 3).reshape(m_count * PP, nr, length // nr)]
    concatenate x4 -> x0, other arithmetic: 20.8 us -> none  [the longest x1 11.8 us: correlate(): return jnp.concatenate([real_part, imag_part], axis=-1)]
    dot_general x2 -> x0, local copies, waits for them, and re-layouts: 19.9 us -> none  [the longest x1 9.96 us: correlate(): jnp.einsum('jmk,imk->jik', left_both, right_both, preferred_element_type=...]
  transfers between devices with their start and end apart: 2 -> 0, of which waited for: 2 -> 0; matrix products, arithmetic and copies ran while one was open for 8% -> 0% of each run, Pallas kernels for 0% -> 0%
where the time goes in v1:
time: 109 us
  Pallas kernels  87.1 us (80%)
  local copies, waits for them, and re-layouts  11.2 us (10%)
  other arithmetic  5.9 us (5%)
  matrix products  2.59 us (2%)
  between operations  2 us (2%)
    pallas_call x1, Pallas kernels, on_device(): pl.pallas_call(functools.partial(kernel, (nb, nt, m_count, length)), out_...  87.1 us
    transpose x1, local copies, waits for them, and re-layouts, on_device(): x = traces.transpose(1, 2, 0, 3).reshape(m_count, channels, length)  7.54 us
    dot_general x1, matrix products, on_device(): lax.dot_general(cross, inverse, (((1,), (0,)), ((), ())), preferred_eleme...  2.59 us

profile of v1, /device:TPU:0, one launch (start us, length us, event | category | flops | bytes accessed | tf_op | source)
XLA Modules:
  0.0 108.7 jit_solution(15201686389395863101)
XLA Ops:
  0.0 1.3 %fusion.12 = s32[]{:T(128)} fusion(s32[4]{0:T(128)} %param.9, s32[4]{0:T(128)} %param.8, s32[]{:T(128)S(6)} %axis_index.15), kind=kLoop, calls=%fused_computation.32 | loop fusion | flops 11 | bytes 40 | tf_op jit(solution)/shard_map/reduce_sum | solution.py:347
  3.3 0.7 broadcast_in_dim.28
  4.0 0.1 tile.7
  4.1 0.8 constant_dynamic-slice_fusion
  4.9 0.1 copy.27
  5.0 0.1 copy.20
  5.1 0.1 eq.54
  5.2 0.7 convert_bitcast_fusion
  5.9 0.6 convert_element_type.24.valid
  6.5 1.1 fusion
  7.6 0.1 copy.21
  7.7 0.7 copy.29
  8.4 0.9 and_convert_fusion.onehot
  9.3 7.5 %copy.18 = bf16[2,6,256,1024]{3,2,1,0:T(8,128)(2,1)} copy(bf16[2,6,256,1024]{3,0,1,2:T(2,128)(2,1)} %bitcast.14) | data formatting | bytes 12582912 | tf_op jit(solution)/shard_map/transpose | solution.py:345
  16.8 87.1 %cross.1 = f32[2,16,64,256]{3,2,1,0:T(8,128)} custom-call(bf16[12,256,1024]{2,1,0:T(8,128)(2,1)} %bitcast.13, bf16[1024,1024]{1,0:T(8,128)(2,1)} %constant.84.clone.ft_hbm, bf16[8,48,128]{2,1,0:T(8,128)(2,1)} %bitcast.16, bf16[192,768]{1,0:T(8,128)(2,1)} %and_convert_fusion.onehot, f32[12,1,256]{2,1,0:T(1,128)} %convert_element_type.24.valid), custom_call_target="tpu_custom_call" | custom-call | tf_op jit(solution)/shard_map/cross/pallas_call | solution.py:371
  103.9 0.0 copy-start
  103.9 1.9 %convert_element_type.22 = bf16[2,16,64,256]{3,2,1,0:T(8,128)(2,1)S(1)} convert(f32[2,16,64,256]{3,2,1,0:T(8,128)} %cross.1) | non-fusion elementwise | flops 524288 | bytes 3145728 | tf_op jit(solution)/shard_map/convert_element_type | solution.py:407
  105.8 0.3 copy-done
  106.1 2.6 %fusion.13 = f32[2,256,1024]{2,1,0:T(8,128)} fusion(bf16[2,1024,256]{2,1,0:T(8,128)(2,1)S(1)} %bitcast.15, bf16[1024,1024,1]{1,0,2:T(8,128)(2,1)S(1)} %copy-done), kind=kOutput, calls=%fused_computation.34 | convolution fusion | flops 1073741824 | bytes 5242880 | tf_op jit(solution)/shard_map/dot_general | solution.py:408
  (7 shorter events, 0.1 us)
Async XLA Ops:
  103.9 2.2 %copy-start = (bf16[1024,1024,1]{1,0,2:T(8,128)(2,1)S(1)}, bf16[1024,1024,1]{1,0,2:T(8,128)(2,1)}, u32[]{:S(2)}) copy-start(bf16[1024,1024,1]{1,0,2:T(8,128)(2,1)} %constant.88) | copy-start | bytes 6291460

commit v2 on v1

v2 whole, which is shorter than its diff:
```python
import functools
import math

import jax
import jax.numpy as jnp
import ml_dtypes
import numpy as np
from jax import lax
from jax.experimental import pallas as pl
from jax.experimental.pallas import tpu as pltpu
from jax.sharding import PartitionSpec as P

MESH = pl.DeviceIdType.MESH
PP = 4
NP = 4
J = PP * NP
GB = 8
PAIR = 2 * GB
KB = 32
GP = KB // PAIR
RJ = GP * 2 * PAIR
NZ = 7
NY = 9
NT = (((1,), (1,)), ((), ()))


def forward_t(length):
    k = np.arange(length // 2)
    n = np.arange(length)
    a = (k[:, None] * n[None, :] % length) * (2.0 * math.pi / length)
    return np.concatenate([np.cos(a), -np.sin(a)], axis=0).astype(np.float32).astype(ml_dtypes.bfloat16)


def inverse_rows(length, factor):
    bins = length // 2
    k = np.arange(bins)
    t = np.arange(length)
    a = (k[:, None] * t[None, :] % length) * (2.0 * math.pi / length)
    w = np.where(k == 0, 1.0, 2.0)[:, None] * factor
    full = np.stack([w * np.cos(a), -w * np.sin(a)])
    full = full.reshape(2, bins // PAIR, PAIR, length).transpose(1, 0, 2, 3)
    return full.reshape(length, length).astype(np.float32).astype(ml_dtypes.bfloat16)


def kernel(dims, x_hbm, ft_hbm, valid, owner, first, c_out, xv, ftv, w, scale, p, s, slab, xs,
           rsb, keep, rz1, zfl, zfr, zrl, zrr, yfl, yfr, yrl, yrr, zs, rz2,
           x_sem, ft_sem, rs_send, rs_recv, ag_send, fw_send, ag_recv,
           z1_send, z1_recv, zy_send, zfl_recv, zfr_recv, zrl_recv, zrr_recv,
           yy_send, yfl_recv, yfr_recv, yrl_recv, yrr_recv, z2_send, z2_recv):
    nb, nt, segments, length = dims
    m_count = 2 * segments
    bins = length // 2
    channels = c_out.shape[-1]
    ny = nt // 2
    nr = nb // 2
    lanes = length // nr
    b = lax.axis_index("block")
    t = lax.axis_index("tm")
    part = b // 2
    core = b % 2
    y = t // 2
    z = t % 2
    right = (b, (y + 1) % ny * 2 + z)
    left = (b, (y + ny - 1) % ny * 2 + z)
    across = (b, y * 2 + 1 - z)
    sibling = (part * 2 + 1 - core, t)
    yr = (y + 1) % ny
    yl = (y + ny - 1) % ny
    yo = (y + 2) % ny

    def remote(src, dst, send, recv, device):
        return pltpu.make_async_remote_copy(
            src_ref=src, dst_ref=dst, send_sem=send, recv_sem=recv,
            device_id=device, device_id_type=MESH,
        )

    def iota(shape, axis):
        return lax.broadcasted_iota(jnp.int32, shape, axis)

    def loop(count, body, skip=None):
        def step(i, _):
            if skip is None:
                body(i)
            else:
                pl.when(i != skip)(lambda: body(i))
            return 0

        lax.fori_loop(0, count, step, 0)

    def load(g):
        return pltpu.make_async_copy(x_hbm.at[:, g], xv.at[:, g], x_sem.at[g])

    loop(segments, lambda g: load(g).start())
    pltpu.make_async_copy(ft_hbm, ftv, ft_sem).start()

    barrier = pltpu.get_barrier_semaphore()

    def greet(device):
        pl.semaphore_signal(barrier, inc=1, device_id=device, device_id_type=MESH)

    loop(nb, lambda e: greet((e, t)), b)
    for device in (right, left, across):
        greet(device)

    loop(segments, lambda g: load(g).wait())
    start = 0
    for panel in range(NP):
        start = start + jnp.where(owner[panel] == b, first[panel], 0)
    valid_rows = valid[...].reshape(m_count, channels).astype(jnp.float32)
    for q in range(PP):
        good = jnp.sum(
            jnp.where(iota((m_count, channels), 1) == start + q, valid_rows, 0.0),
            axis=1, keepdims=True,
        )
        rows = xv[start + q].reshape(m_count, length).astype(jnp.float32) * good
        rows = jnp.concatenate([rows, jnp.zeros((16 - m_count, length), jnp.float32)], axis=0)
        rows = rows.astype(jnp.bfloat16)
        for r in range(nr):
            slab[r, q // 2, pl.ds(q % 2 * 16, 16), :] = rows[:, r * lanes:(r + 1) * lanes]
    pl.semaphore_wait(barrier, nb - 1 + 3)

    def rs_copy(e):
        return remote(slab.at[e // 2, e % 2], rsb.at[b], rs_send.at[e], rs_recv.at[b], (e, t))

    def rs_arrived(e):
        remote(slab.at[part, core], rsb.at[e], rs_send.at[e], rs_recv.at[e], (e, t)).wait_recv()

    loop(nb, lambda e: rs_copy(e).start(), b)

    order = iota((256, 256), 1) == iota((256, 256), 0) % 128 * 2 + iota((256, 256), 0) // 128
    order = order.astype(jnp.float32).astype(jnp.bfloat16)

    def transform(g):
        halves = []
        for h in range(2):
            mixed = xv[pl.ds(h * 128, 128), g].reshape(256, length)
            halves.append(
                jnp.dot(order, mixed, preferred_element_type=jnp.float32).astype(jnp.bfloat16)
            )
        for v in range(2):
            m = g * 2 + v
            rows = jnp.concatenate([half[v * 128:(v + 1) * 128] for half in halves], axis=0)
            spectrum = lax.dot_general(ftv[...], rows, NT, preferred_element_type=jnp.float32)
            w[m] = spectrum
            energy = jnp.sum(spectrum * spectrum, axis=0, keepdims=True) * (1.0 / length)
            scale[m] = lax.rsqrt(energy + 1e-06) * valid[g, pl.ds(v, 1), :].astype(jnp.float32)

    def transforms(low, high):
        def step(g, _):
            transform(g)
            return 0

        lax.fori_loop(low, high, step, 0)

    pltpu.make_async_copy(ft_hbm, ftv, ft_sem).wait()
    transforms(0, 2)

    rsb[b] = slab[part, core]
    loop(nb, rs_arrived, b)
    shape = (m_count * 2 * NP, nb * 32)
    row, lane = iota(shape, 0), iota(shape, 1)
    wanted = jnp.zeros(shape, jnp.int32)
    for panel in range(NP):
        wanted = jnp.where(row // 2 % NP == panel, owner[panel], wanted)
    choice = (
        (lane // 32 == wanted) & (lane // 16 % 2 == row % 2) & (lane % 16 == row // (2 * NP))
    )
    picked = jnp.dot(
        choice.astype(jnp.float32).astype(jnp.bfloat16), rsb[...].reshape(nb * 32, lanes),
        preferred_element_type=jnp.float32,
    )
    xs[part, core] = picked.astype(jnp.bfloat16)

    def ag_copy(r):
        return remote(xs.at[part, core], xs.at[part, core], ag_send.at[r],
                      ag_recv.at[part, core], (2 * r + core, t))

    def fw_copy(r):
        return remote(xs.at[r, core], xs.at[r, core], fw_send.at[r], ag_recv.at[r, core], sibling)

    def arrived(r, h):
        remote(xs.at[r, h], xs.at[r, h], fw_send.at[r], ag_recv.at[r, h], sibling).wait_recv()

    loop(nr, lambda r: ag_copy(r).start(), part)
    fw_copy(part).start()
    transforms(2, segments - 1)

    def forward(r):
        arrived(r, core)
        fw_copy(r).start()

    loop(nr, forward, part)
    transforms(segments - 1, segments)
    loop(nr, lambda r: arrived(r, 1 - core))

    half_rows = []
    for h in range(2):
        half_rows.append(jnp.concatenate([xs[r, h] for r in range(nr)], axis=1))
        half_rows.append(jnp.zeros((128 - m_count * 2 * NP, length), jnp.bfloat16))
    source_rows = jnp.concatenate(half_rows, axis=0)
    spectrum = lax.dot_general(ftv[...], source_rows, NT, preferred_element_type=jnp.float32)
    energy = jnp.sum(spectrum * spectrum, axis=0, keepdims=True) * (1.0 / length)
    s[...] = spectrum * lax.rsqrt(energy + 1e-06)


    def correlate_group(k0):
        row, lane = iota((128, 256), 0), iota((128, 256), 1)
        channel = lane // 2 % NP * PP + lane // 128 * 2 + lane % 2
        copies = (row // GB == channel).astype(jnp.float32).astype(jnp.bfloat16)
        segment = row // GB == lane // (2 * NP) % 16
        diagonal = row % GB == lane % GB
        stacked = []
        for base in (0, bins):
            tile = s[pl.ds(pl.multiple_of(base + k0, GB), GB), :]
            stacked.append(jnp.where(segment, jnp.concatenate([tile] * 16, axis=0), 0.0))
        stacked = jnp.concatenate(stacked, axis=0).astype(jnp.bfloat16)
        real = lax.dot_general(copies, stacked, NT, preferred_element_type=jnp.float32)
        real = jnp.where(diagonal, real, 0.0)
        imag = jnp.concatenate([-real[:, 128:], real[:, :128]], axis=1)
        left_side = jnp.concatenate([real, imag], axis=0).astype(jnp.bfloat16)
        rows = []
        for base in (0, bins):
            for m in range(m_count):
                tile = w[m, pl.ds(pl.multiple_of(base + k0, GB), GB), :]
                rows.append(tile * scale[m])
            rows.append(jnp.zeros((128 - m_count * GB, channels), jnp.float32))
        right_side = jnp.concatenate(rows, axis=0).astype(jnp.bfloat16)
        return jnp.dot(left_side, right_side, preferred_element_type=jnp.float32)

    def correlate_chunk(c):
        for g in range(GP):
            k0 = c * KB + g * PAIR
            first = correlate_group(k0).reshape(2, J, GB, channels)
            second = correlate_group(k0 + GB).reshape(2, J, GB, channels)
            both = jnp.concatenate([first, second], axis=2).astype(jnp.bfloat16)
            both = both.reshape(2, ny, 2, 2, PAIR, channels)
            for o in range(2):
                p[c, :, :, :, pl.ds((g * 2 + o) * PAIR, PAIR), :] = both[o]

    def z1(n):
        return remote(p.at[n, :, 1 - z], rz1.at[n], z1_send.at[n], z1_recv.at[n], across)

    def ring(parts, n, fl, fr, rl, rr, send, fl_recv, fr_recv, rl_recv, rr_recv):
        def copy(i):
            src, dst, recv, device = (
                lambda: (parts(yo, 0), fl.at[n], fl_recv.at[n], right),
                lambda: (parts(yo, 1), fr.at[n], fr_recv.at[n], left),
                lambda: (parts(yr, 1), rl.at[n, 1], rl_recv.at[n, 1], right),
                lambda: (parts(yl, 0), rr.at[n, 0], rr_recv.at[n, 0], left),
                lambda: (fl.at[n], rl.at[n, 0], rl_recv.at[n, 0], right),
                lambda: (fr.at[n], rr.at[n, 1], rr_recv.at[n, 1], left),
            )[i]()
            return remote(src, dst, send.at[n, i], recv, device)

        return copy

    def add(a, c):
        return (a.astype(jnp.float32) + c.astype(jnp.float32)).astype(jnp.bfloat16)

    def z_ring(n):
        return ring(lambda o, h: rz1.at[n, o, h], n, zfl, zfr, zrl, zrr,
                    zy_send, zfl_recv, zfr_recv, zrl_recv, zrr_recv)

    def y_ring(n):
        return ring(lambda o, h: p.at[NZ + n, o, h], n, yfl, yfr, yrl, yrr,
                    yy_send, yfl_recv, yfr_recv, yrl_recv, yrr_recv)

    def z2(n):
        return remote(zs.at[n], rz2.at[n], z2_send.at[n], z2_recv.at[n], across)

    def slot(n, _):
        @pl.when(n < NZ)
        def _():
            correlate_chunk(n)
            z1(n).start()

        @pl.when(n < NY)
        def _():
            correlate_chunk(NZ + n)
            for i in range(4):
                y_ring(n)(i).start()

        @pl.when((n >= 1) & (n < NY + 1))
        def _():
            k = n - 1
            copies = y_ring(k)
            copies(0).wait_recv()
            yfl[k] = add(yfl[k], p[NZ + k, yr, 0])
            copies(4).start()
            copies(1).wait_recv()
            yfr[k] = add(yfr[k], p[NZ + k, yl, 1])
            copies(5).start()

        @pl.when((n >= 1) & (n < NZ + 1))
        def _():
            k = n - 1
            z1(k).wait_recv()
            rz1[k] = add(rz1[k], p[k, :, z])
            for i in range(4):
                z_ring(k)(i).start()

        @pl.when((n >= 2) & (n < NY + 2))
        def _():
            k = n - 2
            copies = y_ring(k)
            for i in (2, 3, 4, 5):
                copies(i).wait_recv()
            total = (p[NZ + k, y].astype(jnp.float32) + yrl[k].astype(jnp.float32)
                     + yrr[k].astype(jnp.float32))
            zs[k] = jnp.where(z == 0, total[1], total[0]).astype(jnp.bfloat16)
            keep[k] = jnp.where(z == 0, total[0], total[1])
            z2(k).start()

        @pl.when((n >= 2) & (n < NZ + 2))
        def _():
            k = n - 2
            copies = z_ring(k)
            copies(0).wait_recv()
            zfl[k] = add(zfl[k], rz1[k, yr, 0])
            copies(4).start()
            copies(1).wait_recv()
            zfr[k] = add(zfr[k], rz1[k, yl, 1])
            copies(5).start()

        @pl.when((n >= 3) & (n < NZ + 3))
        def _():
            k = n - 3
            copies = z_ring(k)
            for i in (2, 3, 4, 5):
                copies(i).wait_recv()
            c_out[:, k] = (rz1[k, y].astype(jnp.float32) + zrl[k].astype(jnp.float32)
                           + zrr[k].astype(jnp.float32)).astype(jnp.bfloat16)

        @pl.when(n >= 3)
        def _():
            k = n - 3
            z2(k).wait_recv()
            c_out[:, NZ + k] = (keep[k] + rz2[k].astype(jnp.float32)).astype(jnp.bfloat16)

        return 0

    lax.fori_loop(0, NY + 3, slot, 0)

    loop(nb, lambda e: rs_copy(e).wait_send(), b)
    loop(nr, lambda r: ag_copy(r).wait_send(), part)
    loop(nr, lambda r: fw_copy(r).wait_send())

    def drain_z(n):
        z1(n).wait_send()
        for i in range(6):
            z_ring(n)(i).wait_send()

    def drain_y(n):
        z2(n).wait_send()
        for i in range(6):
            y_ring(n)(i).wait_send()

    loop(NZ, drain_z)
    loop(NY, drain_y)


def on_device(traces, valid, panel_owner, panel_start):
    channels, windows_here, segments, length = traces.shape
    m_count = windows_here * segments
    nb = lax.axis_size("block")
    nt = lax.axis_size("tm")
    nr = nb // 2
    ny = nt // 2
    lanes = length // nr
    forward = jnp.asarray(forward_t(length))
    inverse = jnp.asarray(
        inverse_rows(length, 1.0 / math.sqrt(length // 2 * m_count * nt))
    )
    bf16, f32 = jnp.bfloat16, jnp.float32
    dma = pltpu.SemaphoreType.DMA
    vmem = pl.BlockSpec(memory_space=pltpu.VMEM)
    hbm = pl.BlockSpec(memory_space=pl.ANY)
    smem = pl.BlockSpec(memory_space=pltpu.SMEM)
    chunks = NZ + NY
    unit = (RJ, channels)
    cross = pl.pallas_call(
        functools.partial(kernel, (nb, nt, segments, length)),
        out_shape=jax.ShapeDtypeStruct((2, chunks) + unit, bf16),
        in_specs=[hbm, hbm, vmem, smem, smem],
        out_specs=vmem,
        scratch_shapes=[
            pltpu.VMEM((channels, segments, windows_here, length), bf16),
            pltpu.VMEM((length, length), bf16),
            pltpu.VMEM((m_count, length, channels), f32),
            pltpu.VMEM((m_count, 1, channels), f32),
            pltpu.VMEM((chunks, ny, 2, 2) + unit, bf16),
            pltpu.VMEM((length, 256), f32),
            pltpu.VMEM((nr, 2, 32, lanes), bf16),
            pltpu.VMEM((nr, 2, m_count * 2 * NP, lanes), bf16),
            pltpu.VMEM((nb, 32, lanes), bf16),
            pltpu.VMEM((NY, 2) + unit, f32),
            pltpu.VMEM((NZ, ny, 2) + unit, bf16),
            pltpu.VMEM((NZ,) + unit, bf16),
            pltpu.VMEM((NZ,) + unit, bf16),
            pltpu.VMEM((NZ, 2) + unit, bf16),
            pltpu.VMEM((NZ, 2) + unit, bf16),
            pltpu.VMEM((NY, 2) + unit, bf16),
            pltpu.VMEM((NY, 2) + unit, bf16),
            pltpu.VMEM((NY, 2, 2) + unit, bf16),
            pltpu.VMEM((NY, 2, 2) + unit, bf16),
            pltpu.VMEM((NY, 2) + unit, bf16),
            pltpu.VMEM((NY, 2) + unit, bf16),
            dma((segments,)), dma, dma((nb,)), dma((nb,)), dma((nr,)), dma((nr,)), dma((nr, 2)),
            dma((NZ,)), dma((NZ,)),
            dma((NZ, 6)), dma((NZ,)), dma((NZ,)), dma((NZ, 2)), dma((NZ, 2)),
            dma((NY, 6)), dma((NY,)), dma((NY,)), dma((NY, 2)), dma((NY, 2)),
            dma((NY,)), dma((NY,)),
        ],
        compiler_params=pltpu.CompilerParams(
            collective_id=0, has_side_effects=True, vmem_limit_bytes=56 * 2**20
        ),
        name="cross",
    )(traces.transpose(0, 2, 1, 3), forward, valid.transpose(2, 1, 0), panel_owner, panel_start)
    cross = cross.reshape(2, length, channels)
    return lax.dot_general(
        cross, inverse, (((1,), (0,)), ((), ())), preferred_element_type=f32
    )


def solution(mesh):
    in_specs = (P("block", "tm", None, None), P("block", "tm", None), P(), P())
    out_specs = P("tm", "block", None)
    return jax.shard_map(
        on_device, mesh=mesh, in_specs=in_specs, out_specs=out_specs, check_vma=False
    )
```

time: 109 us -> 91.7 us (0.84)
  local copies, waits for them, and re-layouts: 11.2 us -> 0.01 us
  other arithmetic: 5.9 us -> 0 us
  between operations: 2 us -> 0.02 us
  matrix products: 2.59 us -> 3.81 us
    transpose x2 -> x0, local copies, waits for them, and re-layouts: 7.6 us -> none  [the longest x1 7.54 us: on_device(): x = traces.transpose(1, 2, 0, 3).reshape(m_count, channels, length)]
    convert_element_type x3 -> x0, other arithmetic: 3.51 us -> none  [the longest x1 1.88 us: on_device(): cross = cross.reshape(2, length, channels).astype(bf16)]
    reduce_sum x1 -> x0, other arithmetic: 1.31 us -> none  [on_device(): start = jnp.sum(jnp.where(mine, panel_start, 0))]
    dot_general x1, matrix products: 2.59 us -> 3.81 us  [on_device(): lax.dot_general(cross, inverse, (((1,), (0,)), ((), ())), preferred_eleme...]
where the time goes in v2:
time: 91.7 us; the launch traced here: 91.5 us
  Pallas kernels  87.7 us (96%)
  matrix products  3.81 us (4%)
    pallas_call x1, Pallas kernels, on_device(): pl.pallas_call(functools.partial(kernel, (nb, nt, segments, length)), out...  87.7 us
    dot_general x1, matrix products, on_device(): lax.dot_general(cross, inverse, (((1,), (0,)), ((), ())), preferred_eleme...  3.81 us

profile of v2, /device:TPU:0, one launch (start us, length us, event | category | flops | bytes accessed | tf_op | source)
XLA Modules:
  0.0 91.5 jit_solution(6131900329637850585)
XLA Ops:
  0.0 0.0 copy-start
  0.0 87.7 %cross.1 = bf16[2,16,64,256]{3,2,1,0:T(8,128)(2,1)} custom-call(bf16[256,6,2,1024]{3,2,1,0:T(2,128)(2,1)} %bitcast.6, bf16[1024,1024]{1,0:T(8,128)(2,1)} %constant.4.clone.ft_hbm, s32[6,2,256]{2,1,0:T(2,128)} %bitcast.8, s32[4]{0:T(128)} %owner.1, s32[4]{0:T(128)} %first.1), custom_call_target="tpu_custom_call" | custom-call | tf_op jit(solution)/shard_map/cross/pallas_call | solution.py:381
  87.7 0.0 copy-done
  87.7 3.8 %fusion = f32[2,256,1024]{2,1,0:T(8,128)} fusion(bf16[2,1024,256]{2,1,0:T(8,128)(2,1)} %bitcast.7, bf16[1024,1024,1]{1,0,2:T(8,128)(2,1)S(1)} %copy-done), kind=kOutput, calls=%fused_computation | convolution fusion | flops 1073741824 | bytes 5242880 | tf_op jit(solution)/shard_map/dot_general | solution.py:420
Async XLA Ops:
  0.0 87.7 %copy-start = (bf16[1024,1024,1]{1,0,2:T(8,128)(2,1)S(1)}, bf16[1024,1024,1]{1,0,2:T(8,128)(2,1)}, u32[]{:S(2)}) copy-start(bf16[1024,1024,1]{1,0,2:T(8,128)(2,1)} %constant.8) | copy-start | bytes 6291460

commit v3 on v2

--- a/solution.py
+++ b/solution.py
@@ -16,11 +16,14 @@
 J = PP * NP
 GB = 8
 PAIR = 2 * GB
-KB = 32
-GP = KB // PAIR
-RJ = GP * 2 * PAIR
-NZ = 7
-NY = 9
+KB = PAIR
+RJ = 2 * PAIR
+NY = 8
+NW = 12
+PB = 2 * KB
+PIECES = NW * KB // PB
+CAP = 1536
+LAG = (2, 4, 6)
 NT = (((1,), (1,)), ((), ()))
 
 
@@ -43,9 +46,10 @@
 
 
 def kernel(dims, x_hbm, ft_hbm, valid, owner, first, c_out, xv, ftv, w, scale, p, s, slab, xs,
-           rsb, keep, rz1, zfl, zfr, zrl, zrr, yfl, yfr, yrl, yrr, zs, rz2,
+           rsb, valid2, pos, choose, choose2, pick, packed, packed2, w2, sb, sb2,
+           keep, yfl, yfr, yrl, yrr, zs, rz2,
            x_sem, ft_sem, rs_send, rs_recv, ag_send, fw_send, ag_recv,
-           z1_send, z1_recv, zy_send, zfl_recv, zfr_recv, zrl_recv, zrr_recv,
+           v_send, v_recv, pk_send, pk_recv, sb_send, sb_recv,
            yy_send, yfl_recv, yfr_recv, yrl_recv, yrr_recv, z2_send, z2_recv):
     nb, nt, segments, length = dims
     m_count = 2 * segments
@@ -126,6 +130,8 @@
         remote(slab.at[part, core], rsb.at[e], rs_send.at[e], rs_recv.at[e], (e, t)).wait_recv()
 
     loop(nb, lambda e: rs_copy(e).start(), b)
+    v_copy = remote(valid, valid2, v_send, v_recv, across)
+    v_copy.start()
 
     order = iota((256, 256), 1) == iota((256, 256), 0) % 128 * 2 + iota((256, 256), 0) // 128
     order = order.astype(jnp.float32).astype(jnp.bfloat16)
@@ -153,7 +159,7 @@
         lax.fori_loop(low, high, step, 0)
 
     pltpu.make_async_copy(ft_hbm, ftv, ft_sem).wait()
-    transforms(0, 2)
+    transforms(0, 4)
 
     rsb[b] = slab[part, core]
     loop(nb, rs_arrived, b)
@@ -183,14 +189,70 @@
 
     loop(nr, lambda r: ag_copy(r).start(), part)
     fw_copy(part).start()
-    transforms(2, segments - 1)
+    transforms(4, segments)
 
     def forward(r):
         arrived(r, core)
         fw_copy(r).start()
 
     loop(nr, forward, part)
-    transforms(segments - 1, segments)
+
+    places = CAP // 256
+
+    def build(valid_ref, choose_ref):
+        good = valid_ref[...].reshape(m_count, channels).astype(jnp.float32)
+        good = jnp.concatenate([good, jnp.zeros((16 - m_count, channels), jnp.float32)], axis=0)
+        narrow = good.astype(jnp.bfloat16)
+        before = (iota((channels, channels), 0) < iota((channels, channels), 1))
+        before = before.astype(jnp.float32).astype(jnp.bfloat16)
+        rank = jnp.dot(narrow, before, preferred_element_type=jnp.float32)
+        above = (iota((16, 16), 1) < iota((16, 16), 0)).astype(jnp.float32).astype(jnp.bfloat16)
+        rank = rank + jnp.sum(
+            jnp.dot(above, narrow, preferred_element_type=jnp.float32), axis=1, keepdims=True
+        )
+        rank = jnp.where(good > 0.0, rank, -1.0)
+        for m in range(m_count):
+            pos[m] = rank[m:m + 1]
+
+        def body(m):
+            number = iota((256, channels), 0).astype(jnp.float32)
+            for c in range(places):
+                hit = jnp.where(number + 256.0 * c == pos[m], 1.0, 0.0).astype(jnp.bfloat16)
+                choose_ref[c, :, pl.ds(pl.multiple_of(m * channels, channels), channels)] = hit
+
+        loop(m_count, body)
+
+    def w_bin(half, i):
+        return NY * KB + half * (NW * KB) + i * PB
+
+    def pack(i):
+        for m in range(m_count):
+            rows = []
+            for piece in range(2):
+                for base in (0, bins):
+                    k0 = pl.multiple_of(base + w_bin(1 - z, i + piece), PB)
+                    rows.append(w[m, pl.ds(k0, PB), :] * scale[m])
+            pick[:, m * channels:(m + 1) * channels] = (
+                jnp.concatenate(rows, axis=0).astype(jnp.bfloat16)
+            )
+
+        def body(c):
+            part_c = lax.dot_general(pick[...], choose[c], NT, preferred_element_type=jnp.float32)
+            part_c = part_c.astype(jnp.bfloat16).reshape(2, 2 * PB, 256)
+            packed[pl.ds(i, 2), :, pl.ds(pl.multiple_of(c * 256, 256), 256)] = part_c
+
+        loop(places, body)
+
+    def pk_copy(i):
+        return remote(packed.at[i], packed2.at[i], pk_send.at[i], pk_recv.at[i], across)
+
+    def sb_copy(i):
+        return remote(sb.at[i], sb2.at[i], sb_send.at[i], sb_recv.at[i], across)
+
+    build(valid, choose)
+    pack(0)
+    pk_copy(0).start()
+    pk_copy(1).start()
     loop(nr, lambda r: arrived(r, 1 - core))
 
     half_rows = []
@@ -202,161 +264,223 @@
     energy = jnp.sum(spectrum * spectrum, axis=0, keepdims=True) * (1.0 / length)
     s[...] = spectrum * lax.rsqrt(energy + 1e-06)
 
-
-    def correlate_group(k0):
+    def narrow_sources(i):
+        for o, base in enumerate((0, bins)):
+            k0 = pl.multiple_of(base + w_bin(1 - z, i), PB)
+            sb[i, o] = s[pl.ds(k0, PB), :].astype(jnp.bfloat16)
+
+    loop(PIECES, narrow_sources)
+    sb_copy(0).start()
+    sb_copy(1).start()
+
+
+    def source_matrix(real_tile, imag_tile):
         row, lane = iota((128, 256), 0), iota((128, 256), 1)
         channel = lane // 2 % NP * PP + lane // 128 * 2 + lane % 2
         copies = (row // GB == channel).astype(jnp.float32).astype(jnp.bfloat16)
         segment = row // GB == lane // (2 * NP) % 16
         diagonal = row % GB == lane % GB
-        stacked = []
-        for base in (0, bins):
-            tile = s[pl.ds(pl.multiple_of(base + k0, GB), GB), :]
-            stacked.append(jnp.where(segment, jnp.concatenate([tile] * 16, axis=0), 0.0))
-        stacked = jnp.concatenate(stacked, axis=0).astype(jnp.bfloat16)
+        stacked = jnp.concatenate(
+            [jnp.where(segment, jnp.concatenate([tile] * 16, axis=0), 0.0)
+             for tile in (real_tile, imag_tile)], axis=0,
+        ).astype(jnp.bfloat16)
         real = lax.dot_general(copies, stacked, NT, preferred_element_type=jnp.float32)
         real = jnp.where(diagonal, real, 0.0)
         imag = jnp.concatenate([-real[:, 128:], real[:, :128]], axis=1)
-        left_side = jnp.concatenate([real, imag], axis=0).astype(jnp.bfloat16)
+        return jnp.concatenate([real, imag], axis=0).astype(jnp.bfloat16)
+
+    def channel_matrix(tile):
         rows = []
-        for base in (0, bins):
-            for m in range(m_count):
-                tile = w[m, pl.ds(pl.multiple_of(base + k0, GB), GB), :]
-                rows.append(tile * scale[m])
+        for o in range(2):
+            rows += [tile(o, m) for m in range(m_count)]
             rows.append(jnp.zeros((128 - m_count * GB, channels), jnp.float32))
-        right_side = jnp.concatenate(rows, axis=0).astype(jnp.bfloat16)
-        return jnp.dot(left_side, right_side, preferred_element_type=jnp.float32)
-
-    def correlate_chunk(c):
-        for g in range(GP):
-            k0 = c * KB + g * PAIR
-            first = correlate_group(k0).reshape(2, J, GB, channels)
-            second = correlate_group(k0 + GB).reshape(2, J, GB, channels)
-            both = jnp.concatenate([first, second], axis=2).astype(jnp.bfloat16)
-            both = both.reshape(2, ny, 2, 2, PAIR, channels)
-            for o in range(2):
-                p[c, :, :, :, pl.ds((g * 2 + o) * PAIR, PAIR), :] = both[o]
-
-    def z1(n):
-        return remote(p.at[n, :, 1 - z], rz1.at[n], z1_send.at[n], z1_recv.at[n], across)
-
-    def ring(parts, n, fl, fr, rl, rr, send, fl_recv, fr_recv, rl_recv, rr_recv):
+        return jnp.concatenate(rows, axis=0).astype(jnp.bfloat16)
+
+    def own_tile(k0):
+        def tile(o, m):
+            return w[m, pl.ds(pl.multiple_of(o * bins + k0, GB), GB), :] * scale[m]
+
+        return tile
+
+    def own_source(o, k0):
+        return s[pl.ds(pl.multiple_of(o * bins + k0, GB), GB), :]
+
+    def store_chunk(n, groups):
+        groups = [g.reshape(2, J, GB, channels) for g in groups]
+        both = jnp.concatenate(groups, axis=2).astype(jnp.bfloat16)
+        both = both.reshape(2, ny, 2, 2, PAIR, channels)
+        for o in range(2):
+            p[n, :, :, :, pl.ds(o * PAIR, PAIR), :] = both[o]
+
+    def correlate_own(n):
+        groups = []
+        for g in range(2):
+            k0 = n * KB + g * GB
+            groups.append(jnp.dot(
+                source_matrix(own_source(0, k0), own_source(1, k0)),
+                channel_matrix(own_tile(k0)), preferred_element_type=jnp.float32,
+            ))
+        store_chunk(n, groups)
+
+    def correlate_both(k):
+        i, half = k // 2, k % 2
+        far = [sb2[i, o, pl.ds(pl.multiple_of(half * PAIR, PAIR), PAIR), :].astype(jnp.float32)
+               for o in range(2)]
+        groups = []
+        for g in range(2):
+            k0 = w_bin(z, 0) + k * KB + g * GB
+            near = source_matrix(own_source(0, k0), own_source(1, k0))
+            other = source_matrix(*[f[g * GB:(g + 1) * GB] for f in far])
+
+            def far_tile(o, m):
+                row = (i % 2 * 2 + o) * PB + half * PAIR + g * GB
+                return w2[m, pl.ds(pl.multiple_of(row, GB), GB), :]
+
+            groups.append(jnp.dot(
+                jnp.concatenate([near, other], axis=1),
+                jnp.concatenate(
+                    [channel_matrix(own_tile(k0)), channel_matrix(far_tile)], axis=0
+                ),
+                preferred_element_type=jnp.float32,
+            ))
+        store_chunk(NY + k, groups)
+
+    def unpack(i):
+        for piece in range(2):
+            pk_copy(i + piece).wait_recv()
+            sb_copy(i + piece).wait_recv()
+        rows = packed2[pl.ds(i, 2)].reshape(4 * PB, CAP)
+
+        def body(m):
+            lanes_m = pl.ds(pl.multiple_of(m * channels, channels), channels)
+            side = choose2[:, :, lanes_m].reshape(CAP, channels)
+            w2[m] = jnp.dot(rows, side, preferred_element_type=jnp.float32)
+
+        loop(m_count, body)
+
+    def ring(n):
         def copy(i):
             src, dst, recv, device = (
-                lambda: (parts(yo, 0), fl.at[n], fl_recv.at[n], right),
-                lambda: (parts(yo, 1), fr.at[n], fr_recv.at[n], left),
-                lambda: (parts(yr, 1), rl.at[n, 1], rl_recv.at[n, 1], right),
-                lambda: (parts(yl, 0), rr.at[n, 0], rr_recv.at[n, 0], left),
-                lambda: (fl.at[n], rl.at[n, 0], rl_recv.at[n, 0], right),
-                lambda: (fr.at[n], rr.at[n, 1], rr_recv.at[n, 1], left),
+                lambda: (p.at[n, yo, 0], yfl.at[n], yfl_recv.at[n], right),
+                lambda: (p.at[n, yo, 1], yfr.at[n], yfr_recv.at[n], left),
+                lambda: (p.at[n, yr, 1], yrl.at[n, 1], yrl_recv.at[n, 1], right),
+                lambda: (p.at[n, yl, 0], yrr.at[n, 0], yrr_recv.at[n, 0], left),
+                lambda: (yfl.at[n], yrl.at[n, 0], yrl_recv.at[n, 0], right),
+                lambda: (yfr.at[n], yrr.at[n, 1], yrr_recv.at[n, 1], left),
             )[i]()
-            return remote(src, dst, send.at[n, i], recv, device)
+            return remote(src, dst, yy_send.at[n, i], recv, device)
 
         return copy
 
     def add(a, c):
         return (a.astype(jnp.float32) + c.astype(jnp.float32)).astype(jnp.bfloat16)
 
-    def z_ring(n):
-        return ring(lambda o, h: rz1.at[n, o, h], n, zfl, zfr, zrl, zrr,
-                    zy_send, zfl_recv, zfr_recv, zrl_recv, zrr_recv)
-
-    def y_ring(n):
-        return ring(lambda o, h: p.at[NZ + n, o, h], n, yfl, yfr, yrl, yrr,
-                    yy_send, yfl_recv, yfr_recv, yrl_recv, yrr_recv)
-
     def z2(n):
         return remote(zs.at[n], rz2.at[n], z2_send.at[n], z2_recv.at[n], across)
 
+    def ring_pass(n):
+        copies = ring(n)
+        copies(0).wait_recv()
+        yfl[n] = add(yfl[n], p[n, yr, 0])
+        copies(4).start()
+        copies(1).wait_recv()
+        yfr[n] = add(yfr[n], p[n, yl, 1])
+        copies(5).start()
+
+    def ring_sum(n):
+        copies = ring(n)
+        for i in (2, 3, 4, 5):
+            copies(i).wait_recv()
+        total = (p[n, y].astype(jnp.float32) + yrl[n].astype(jnp.float32)
+                 + yrr[n].astype(jnp.float32))
+        zs[n] = jnp.where(z == 0, total[1], total[0]).astype(jnp.bfloat16)
+        z2(n).start()
+        mine = jnp.where(z == 0, total[0], total[1])
+
+        @pl.when(n < NY)
+        def _():
+            keep[n] = mine
+
+        @pl.when(n >= NY)
+        def _():
+            c_out[:, n + z * NW] = mine.astype(jnp.bfloat16)
+
+    def ring_end(n):
+        z2(n).wait_recv()
+
+        @pl.when(n < NY)
+        def _():
+            c_out[:, n] = (keep[n] + rz2[n].astype(jnp.float32)).astype(jnp.bfloat16)
+
+        @pl.when(n >= NY)
+        def _():
+            c_out[:, n + (1 - z) * NW] = rz2[n]
+
+    def pack_rest(j):
+        i = 2 * j + 2
+        pack(i)
+        for piece in range(2):
+            pk_copy(i + piece).start()
+            sb_copy(i + piece).start()
+
+    chunks = NY + NW
+
     def slot(n, _):
-        @pl.when(n < NZ)
-        def _():
-            correlate_chunk(n)
-            z1(n).start()
+        def at(lag, body):
+            pl.when((n >= lag) & (n < chunks + lag))(lambda: body(n - lag))
+
+        at(LAG[0], ring_pass)
+        at(LAG[1], ring_sum)
+        at(LAG[2], ring_end)
+
+        @pl.when(n == 2)
+        def _():
+            loop(PIECES // 2 - 1, pack_rest)
+
+        @pl.when(n == NY - 2)
+        def _():
+            v_copy.wait_recv()
+            build(valid2, choose2)
 
         @pl.when(n < NY)
         def _():
-            correlate_chunk(NZ + n)
+            correlate_own(n)
+
+        @pl.when((n >= NY) & (n < chunks) & ((n - NY) % 4 == 0))
+        def _():
+            unpack((n - NY) // 2)
+
+        @pl.when((n >= NY) & (n < chunks))
+        def _():
+            correlate_both(n - NY)
+
+        @pl.when(n < chunks)
+        def _():
             for i in range(4):
-                y_ring(n)(i).start()
-
-        @pl.when((n >= 1) & (n < NY + 1))
-        def _():
-            k = n - 1
-            copies = y_ring(k)
-            copies(0).wait_recv()
-            yfl[k] = add(yfl[k], p[NZ + k, yr, 0])
-            copies(4).start()
-            copies(1).wait_recv()
-            yfr[k] = add(yfr[k], p[NZ + k, yl, 1])
-            copies(5).start()
-
-        @pl.when((n >= 1) & (n < NZ + 1))
-        def _():
-            k = n - 1
-            z1(k).wait_recv()
-            rz1[k] = add(rz1[k], p[k, :, z])
-            for i in range(4):
-                z_ring(k)(i).start()
-
-        @pl.when((n >= 2) & (n < NY + 2))
-        def _():
-            k = n - 2
-            copies = y_ring(k)
-            for i in (2, 3, 4, 5):
-                copies(i).wait_recv()
-            total = (p[NZ + k, y].astype(jnp.float32) + yrl[k].astype(jnp.float32)
-                     + yrr[k].astype(jnp.float32))
-            zs[k] = jnp.where(z == 0, total[1], total[0]).astype(jnp.bfloat16)
-            keep[k] = jnp.where(z == 0, total[0], total[1])
-            z2(k).start()
-
-        @pl.when((n >= 2) & (n < NZ + 2))
-        def _():
-            k = n - 2
-            copies = z_ring(k)
-            copies(0).wait_recv()
-            zfl[k] = add(zfl[k], rz1[k, yr, 0])
-            copies(4).start()
-            copies(1).wait_recv()
-            zfr[k] = add(zfr[k], rz1[k, yl, 1])
-            copies(5).start()
-
-        @pl.when((n >= 3) & (n < NZ + 3))
-        def _():
-            k = n - 3
-            copies = z_ring(k)
-            for i in (2, 3, 4, 5):
-                copies(i).wait_recv()
-            c_out[:, k] = (rz1[k, y].astype(jnp.float32) + zrl[k].astype(jnp.float32)
-                           + zrr[k].astype(jnp.float32)).astype(jnp.bfloat16)
-
-        @pl.when(n >= 3)
-        def _():
-            k = n - 3
-            z2(k).wait_recv()
-            c_out[:, NZ + k] = (keep[k] + rz2[k].astype(jnp.float32)).astype(jnp.bfloat16)
+                ring(n)(i).start()
 
         return 0
 
-    lax.fori_loop(0, NY + 3, slot, 0)
+    lax.fori_loop(0, chunks + max(LAG), slot, 0)
 
     loop(nb, lambda e: rs_copy(e).wait_send(), b)
     loop(nr, lambda r: ag_copy(r).wait_send(), part)
     loop(nr, lambda r: fw_copy(r).wait_send())
 
-    def drain_z(n):
-        z1(n).wait_send()
-        for i in range(6):
-            z_ring(n)(i).wait_send()
-
-    def drain_y(n):
+    v_copy.wait_send()
+
+    def drain_piece(i):
+        pk_copy(i).wait_send()
+        sb_copy(i).wait_send()
+
+    loop(PIECES, drain_piece)
+
+    def drain(n):
         z2(n).wait_send()
         for i in range(6):
-            y_ring(n)(i).wait_send()
-
-    loop(NZ, drain_z)
-    loop(NY, drain_y)
+            ring(n)(i).wait_send()
+
+    loop(chunks, drain)
 
 
 def on_device(traces, valid, panel_owner, panel_start):
@@ -376,7 +500,8 @@
     vmem = pl.BlockSpec(memory_space=pltpu.VMEM)
     hbm = pl.BlockSpec(memory_space=pl.ANY)
     smem = pl.BlockSpec(memory_space=pltpu.SMEM)
-    chunks = NZ + NY
+    chunks = NY + 2 * NW
+    work = NY + NW
     unit = (RJ, channels)
     cross = pl.pallas_call(
         functools.partial(kernel, (nb, nt, segments, length)),
@@ -388,31 +513,35 @@
             pltpu.VMEM((length, length), bf16),
             pltpu.VMEM((m_count, length, channels), f32),
             pltpu.VMEM((m_count, 1, channels), f32),
-            pltpu.VMEM((chunks, ny, 2, 2) + unit, bf16),
+            pltpu.VMEM((work, ny, 2, 2) + unit, bf16),
             pltpu.VMEM((length, 256), f32),
             pltpu.VMEM((nr, 2, 32, lanes), bf16),
             pltpu.VMEM((nr, 2, m_count * 2 * NP, lanes), bf16),
             pltpu.VMEM((nb, 32, lanes), bf16),
+            pltpu.VMEM((segments, windows_here, channels), jnp.int32),
+            pltpu.VMEM((m_count, 1, channels), f32),
+            pltpu.VMEM((CAP // 256, 256, m_count * channels), bf16),
+            pltpu.VMEM((CAP // 256, 256, m_count * channels), bf16),
+            pltpu.VMEM((4 * PB, m_count * channels), bf16),
+            pltpu.VMEM((PIECES, 2 * PB, CAP), bf16),
+            pltpu.VMEM((PIECES, 2 * PB, CAP), bf16),
+            pltpu.VMEM((m_count, 4 * PB, channels), f32),
+            pltpu.VMEM((PIECES, 2, PB, 256), bf16),
+            pltpu.VMEM((PIECES, 2, PB, 256), bf16),
             pltpu.VMEM((NY, 2) + unit, f32),
-            pltpu.VMEM((NZ, ny, 2) + unit, bf16),
-            pltpu.VMEM((NZ,) + unit, bf16),
-            pltpu.VMEM((NZ,) + unit, bf16),
-            pltpu.VMEM((NZ, 2) + unit, bf16),
-            pltpu.VMEM((NZ, 2) + unit, bf16),
-            pltpu.VMEM((NY, 2) + unit, bf16),
-            pltpu.VMEM((NY, 2) + unit, bf16),
-            pltpu.VMEM((NY, 2, 2) + unit, bf16),
-            pltpu.VMEM((NY, 2, 2) + unit, bf16),
-            pltpu.VMEM((NY, 2) + unit, bf16),
-            pltpu.VMEM((NY, 2) + unit, bf16),
+            pltpu.VMEM((work, 2) + unit, bf16),
+            pltpu.VMEM((work, 2) + unit, bf16),
+            pltpu.VMEM((work, 2, 2) + unit, bf16),
+            pltpu.VMEM((work, 2, 2) + unit, bf16),
+            pltpu.VMEM((work, 2) + unit, bf16),
+            pltpu.VMEM((work, 2) + unit, bf16),
             dma((segments,)), dma, dma((nb,)), dma((nb,)), dma((nr,)), dma((nr,)), dma((nr, 2)),
-            dma((NZ,)), dma((NZ,)),
-            dma((NZ, 6)), dma((NZ,)), dma((NZ,)), dma((NZ, 2)), dma((NZ, 2)),
-            dma((NY, 6)), dma((NY,)), dma((NY,)), dma((NY, 2)), dma((NY, 2)),
-            dma((NY,)), dma((NY,)),
+            dma, dma, dma((PIECES,)), dma((PIECES,)), dma((PIECES,)), dma((PIECES,)),
+            dma((work, 6)), dma((work,)), dma((work,)), dma((work, 2)), dma((work, 2)),
+            dma((work,)), dma((work,)),
         ],
         compiler_params=pltpu.CompilerParams(
-            collective_id=0, has_side_effects=True, vmem_limit_bytes=56 * 2**20
+            collective_id=0, has_side_effects=True, vmem_limit_bytes=60 * 2**20
         ),
         name="cross",
     )(traces.transpose(0, 2, 1, 3), forward, valid.transpose(2, 1, 0), panel_owner, panel_start)

time: 91.7 us -> 117 us (1.28)
  Pallas kernels: 87.7 us -> 112 us
    pallas_call x1, Pallas kernels: 87.7 us -> 112 us  [on_device(): pl.pallas_call(functools.partial(kernel, (nb, nt, segments, length)), out...]
where the time goes in v3:
time: 117 us; the launch traced here: 116 us
  Pallas kernels  112 us (96%)
  matrix products  3.81 us (3%)
    pallas_call x1, Pallas kernels, on_device(): pl.pallas_call(functools.partial(kernel, (nb, nt, segments, length)), out...  112 us
    dot_general x1, matrix products, on_device(): lax.dot_general(cross, inverse, (((1,), (0,)), ((), ())), preferred_eleme...  3.81 us

profile of v3, /device:TPU:0, one launch (start us, length us, event | category | flops | bytes accessed | tf_op | source)
XLA Modules:
  0.0 116.0 jit_solution(15892359444288225463)
XLA Ops:
  0.0 0.0 copy-start
  0.0 112.1 %cross.1 = bf16[2,32,32,256]{3,2,1,0:T(8,128)(2,1)} custom-call(bf16[256,6,2,1024]{3,2,1,0:T(2,128)(2,1)} %bitcast.6, bf16[1024,1024]{1,0:T(8,128)(2,1)} %constant.4.clone.ft_hbm, s32[6,2,256]{2,1,0:T(2,128)} %bitcast.8, s32[4]{0:T(128)} %owner.1, s32[4]{0:T(128)} %first.1), custom_call_target="tpu_custom_call" | custom-call | tf_op jit(solution)/shard_map/cross/pallas_call | solution.py:506
  112.1 0.0 copy-done
  112.1 3.8 %fusion = f32[2,256,1024]{2,1,0:T(8,128)} fusion(bf16[2,1024,256]{2,1,0:T(8,128)(2,1)} %bitcast.7, bf16[1024,1024,1]{1,0,2:T(8,128)(2,1)S(1)} %copy-done), kind=kOutput, calls=%fused_computation | convolution fusion | flops 1073741824 | bytes 5242880 | tf_op jit(solution)/shard_map/dot_general | solution.py:549
Async XLA Ops:
  0.0 112.1 %copy-start = (bf16[1024,1024,1]{1,0,2:T(8,128)(2,1)S(1)}, bf16[1024,1024,1]{1,0,2:T(8,128)(2,1)}, u32[]{:S(2)}) copy-start(bf16[1024,1024,1]{1,0,2:T(8,128)(2,1)} %constant.8) | copy-start | bytes 6291460

commit v4 on v3

--- a/solution.py
+++ b/solution.py
@@ -18,12 +18,12 @@
 PAIR = 2 * GB
 KB = PAIR
 RJ = 2 * PAIR
-NY = 8
-NW = 12
+NY = 4
+NW = 14
 PB = 2 * KB
 PIECES = NW * KB // PB
 CAP = 1536
-LAG = (2, 4, 6)
+LAG = (3, 6, 20)
 NT = (((1,), (1,)), ((), ()))
 
 
@@ -225,21 +225,23 @@
     def w_bin(half, i):
         return NY * KB + half * (NW * KB) + i * PB
 
-    def pack(i):
+    def pack(i, count):
         for m in range(m_count):
             rows = []
-            for piece in range(2):
+            for piece in range(count):
                 for base in (0, bins):
                     k0 = pl.multiple_of(base + w_bin(1 - z, i + piece), PB)
                     rows.append(w[m, pl.ds(k0, PB), :] * scale[m])
-            pick[:, m * channels:(m + 1) * channels] = (
+            pick[0:count * 2 * PB, m * channels:(m + 1) * channels] = (
                 jnp.concatenate(rows, axis=0).astype(jnp.bfloat16)
             )
 
         def body(c):
-            part_c = lax.dot_general(pick[...], choose[c], NT, preferred_element_type=jnp.float32)
-            part_c = part_c.astype(jnp.bfloat16).reshape(2, 2 * PB, 256)
-            packed[pl.ds(i, 2), :, pl.ds(pl.multiple_of(c * 256, 256), 256)] = part_c
+            part_c = lax.dot_general(
+                pick[0:count * 2 * PB, :], choose[c], NT, preferred_element_type=jnp.float32
+            )
+            part_c = part_c.astype(jnp.bfloat16).reshape(count, 2 * PB, 256)
+            packed[i:i + count, :, pl.ds(pl.multiple_of(c * 256, 256), 256)] = part_c
 
         loop(places, body)
 
@@ -250,7 +252,7 @@
         return remote(sb.at[i], sb2.at[i], sb_send.at[i], sb_recv.at[i], across)
 
     build(valid, choose)
-    pack(0)
+    pack(0, 2)
     pk_copy(0).start()
     pk_copy(1).start()
     loop(nr, lambda r: arrived(r, 1 - core))
@@ -333,7 +335,7 @@
             other = source_matrix(*[f[g * GB:(g + 1) * GB] for f in far])
 
             def far_tile(o, m):
-                row = (i % 2 * 2 + o) * PB + half * PAIR + g * GB
+                row = ((i + 1) % 2 * 2 + o) * PB + half * PAIR + g * GB
                 return w2[m, pl.ds(pl.multiple_of(row, GB), GB), :]
 
             groups.append(jnp.dot(
@@ -345,16 +347,18 @@
             ))
         store_chunk(NY + k, groups)
 
-    def unpack(i):
-        for piece in range(2):
+    def unpack(i, count):
+        for piece in range(count):
             pk_copy(i + piece).wait_recv()
             sb_copy(i + piece).wait_recv()
-        rows = packed2[pl.ds(i, 2)].reshape(4 * PB, CAP)
+        rows = packed2[pl.ds(i, count)].reshape(count * 2 * PB, CAP)
 
         def body(m):
             lanes_m = pl.ds(pl.multiple_of(m * channels, channels), channels)
             side = choose2[:, :, lanes_m].reshape(CAP, channels)
-            w2[m] = jnp.dot(rows, side, preferred_element_type=jnp.float32)
+            w2[m, (2 - count) * 2 * PB:4 * PB] = jnp.dot(
+                rows, side, preferred_element_type=jnp.float32
+            )
 
         loop(m_count, body)
 
@@ -416,28 +420,24 @@
         def _():
             c_out[:, n + (1 - z) * NW] = rz2[n]
 
-    def pack_rest(j):
-        i = 2 * j + 2
-        pack(i)
-        for piece in range(2):
-            pk_copy(i + piece).start()
-            sb_copy(i + piece).start()
-
     chunks = NY + NW
 
     def slot(n, _):
         def at(lag, body):
             pl.when((n >= lag) & (n < chunks + lag))(lambda: body(n - lag))
 
+        @pl.when(n == NY - 1)
+        def _():
+            pack(2, PIECES - 2)
+            for i in range(2, PIECES):
+                pk_copy(i).start()
+                sb_copy(i).start()
+
         at(LAG[0], ring_pass)
         at(LAG[1], ring_sum)
         at(LAG[2], ring_end)
 
-        @pl.when(n == 2)
-        def _():
-            loop(PIECES // 2 - 1, pack_rest)
-
-        @pl.when(n == NY - 2)
+        @pl.when(n == NY)
         def _():
             v_copy.wait_recv()
             build(valid2, choose2)
@@ -446,9 +446,13 @@
         def _():
             correlate_own(n)
 
-        @pl.when((n >= NY) & (n < chunks) & ((n - NY) % 4 == 0))
-        def _():
-            unpack((n - NY) // 2)
+        @pl.when(n == NY)
+        def _():
+            unpack(0, 1)
+
+        @pl.when((n > NY) & (n < chunks) & ((n - NY) % 4 == 2))
+        def _():
+            unpack((n - NY) // 2, 2)
 
         @pl.when((n >= NY) & (n < chunks))
         def _():
@@ -522,7 +526,7 @@
             pltpu.VMEM((m_count, 1, channels), f32),
             pltpu.VMEM((CAP // 256, 256, m_count * channels), bf16),
             pltpu.VMEM((CAP // 256, 256, m_count * channels), bf16),
-            pltpu.VMEM((4 * PB, m_count * channels), bf16),
+            pltpu.VMEM(((PIECES - 2) * 2 * PB, m_count * channels), bf16),
             pltpu.VMEM((PIECES, 2 * PB, CAP), bf16),
             pltpu.VMEM((PIECES, 2 * PB, CAP), bf16),
             pltpu.VMEM((m_count, 4 * PB, channels), f32),

time: 117 us -> 90.1 us (0.77)
  Pallas kernels: 112 us -> 86.1 us
    pallas_call x1, Pallas kernels: 112 us -> 86.1 us  [on_device(): pl.pallas_call(functools.partial(kernel, (nb, nt, segments, length)), out...]
where the time goes in v4:
time: 90.1 us; the launch traced here: 90 us
  Pallas kernels  86.1 us (96%)
  matrix products  3.81 us (4%)
    pallas_call x1, Pallas kernels, on_device(): pl.pallas_call(functools.partial(kernel, (nb, nt, segments, length)), out...  86.1 us
    dot_general x1, matrix products, on_device(): lax.dot_general(cross, inverse, (((1,), (0,)), ((), ())), preferred_eleme...  3.81 us

profile of v4, /device:TPU:0, one launch (start us, length us, event | category | flops | bytes accessed | tf_op | source)
XLA Modules:
  0.0 90.0 jit_solution(2722756026031364528)
XLA Ops:
  0.0 0.0 copy-start
  0.0 86.1 %cross.1 = bf16[2,32,32,256]{3,2,1,0:T(8,128)(2,1)} custom-call(bf16[256,6,2,1024]{3,2,1,0:T(2,128)(2,1)} %bitcast.6, bf16[1024,1024]{1,0:T(8,128)(2,1)} %constant.4.clone.ft_hbm, s32[6,2,256]{2,1,0:T(2,128)} %bitcast.8, s32[4]{0:T(128)} %owner.1, s32[4]{0:T(128)} %first.1), custom_call_target="tpu_custom_call" | custom-call | tf_op jit(solution)/shard_map/cross/pallas_call | solution.py:510
  86.2 0.0 copy-done
  86.2 3.8 %fusion = f32[2,256,1024]{2,1,0:T(8,128)} fusion(bf16[2,1024,256]{2,1,0:T(8,128)(2,1)} %bitcast.7, bf16[1024,1024,1]{1,0,2:T(8,128)(2,1)S(1)} %copy-done), kind=kOutput, calls=%fused_computation | convolution fusion | flops 1073741824 | bytes 5242880 | tf_op jit(solution)/shard_map/dot_general | solution.py:553
Async XLA Ops:
  0.0 86.2 %copy-start = (bf16[1024,1024,1]{1,0,2:T(8,128)(2,1)S(1)}, bf16[1024,1024,1]{1,0,2:T(8,128)(2,1)}, u32[]{:S(2)}) copy-start(bf16[1024,1024,1]{1,0,2:T(8,128)(2,1)} %constant.8) | copy-start | bytes 6291460

commit v5 on v4

--- a/solution.py
+++ b/solution.py
@@ -18,12 +18,12 @@
 PAIR = 2 * GB
 KB = PAIR
 RJ = 2 * PAIR
-NY = 4
-NW = 14
+NY = 8
+NW = 12
 PB = 2 * KB
 PIECES = NW * KB // PB
 CAP = 1536
-LAG = (3, 6, 20)
+LAG = (3, 6, 17)
 NT = (((1,), (1,)), ((), ()))
 
 
@@ -106,6 +106,48 @@
     for device in (right, left, across):
         greet(device)
 
+    places = CAP // channels
+
+    def lane_block(m):
+        start = m * channels
+        return pl.ds(start if isinstance(m, int) else pl.multiple_of(start, channels), channels)
+
+    def by_segment(body):
+        for m in range(places - 1):
+            body(m, m + 1)
+
+        def step(m, _):
+            body(m, places)
+            return 0
+
+        lax.fori_loop(places - 1, m_count, step, 0)
+
+    def build(valid_ref, choose_ref):
+        good = valid_ref[...].reshape(m_count, channels).astype(jnp.float32)
+        good = jnp.concatenate([good, jnp.zeros((16 - m_count, channels), jnp.float32)], axis=0)
+        narrow = good.astype(jnp.bfloat16)
+        before = (iota((channels, channels), 0) < iota((channels, channels), 1))
+        before = before.astype(jnp.float32).astype(jnp.bfloat16)
+        rank = jnp.dot(narrow, before, preferred_element_type=jnp.float32)
+        above = (iota((16, 16), 1) < iota((16, 16), 0)).astype(jnp.float32).astype(jnp.bfloat16)
+        rank = rank + jnp.sum(
+            jnp.dot(above, narrow, preferred_element_type=jnp.float32), axis=1, keepdims=True
+        )
+        rank = jnp.where(good > 0.0, rank, -1.0)
+        for m in range(m_count):
+            pos[m] = rank[m:m + 1]
+
+        number = iota((256, channels), 0).astype(jnp.float32)
+
+        def fill(m, count):
+            for c in range(count):
+                hit = jnp.where(number + 256.0 * c == pos[m], 1.0, 0.0).astype(jnp.bfloat16)
+                choose_ref[c, :, lane_block(m)] = hit
+
+        by_segment(fill)
+
+    build(valid, choose)
+
     loop(segments, lambda g: load(g).wait())
     start = 0
     for panel in range(NP):
@@ -197,31 +239,6 @@
 
     loop(nr, forward, part)
 
-    places = CAP // 256
-
-    def build(valid_ref, choose_ref):
-        good = valid_ref[...].reshape(m_count, channels).astype(jnp.float32)
-        good = jnp.concatenate([good, jnp.zeros((16 - m_count, channels), jnp.float32)], axis=0)
-        narrow = good.astype(jnp.bfloat16)
-        before = (iota((channels, channels), 0) < iota((channels, channels), 1))
-        before = before.astype(jnp.float32).astype(jnp.bfloat16)
-        rank = jnp.dot(narrow, before, preferred_element_type=jnp.float32)
-        above = (iota((16, 16), 1) < iota((16, 16), 0)).astype(jnp.float32).astype(jnp.bfloat16)
-        rank = rank + jnp.sum(
-            jnp.dot(above, narrow, preferred_element_type=jnp.float32), axis=1, keepdims=True
-        )
-        rank = jnp.where(good > 0.0, rank, -1.0)
-        for m in range(m_count):
-            pos[m] = rank[m:m + 1]
-
-        def body(m):
-            number = iota((256, channels), 0).astype(jnp.float32)
-            for c in range(places):
-                hit = jnp.where(number + 256.0 * c == pos[m], 1.0, 0.0).astype(jnp.bfloat16)
-                choose_ref[c, :, pl.ds(pl.multiple_of(m * channels, channels), channels)] = hit
-
-        loop(m_count, body)
-
     def w_bin(half, i):
         return NY * KB + half * (NW * KB) + i * PB
 
@@ -236,14 +253,13 @@
                 jnp.concatenate(rows, axis=0).astype(jnp.bfloat16)
             )
 
-        def body(c):
+        for c in range(places):
             part_c = lax.dot_general(
-                pick[0:count * 2 * PB, :], choose[c], NT, preferred_element_type=jnp.float32
+                pick[0:count * 2 * PB, c * channels:], choose[c, :, c * channels:], NT,
+                preferred_element_type=jnp.float32,
             )
             part_c = part_c.astype(jnp.bfloat16).reshape(count, 2 * PB, 256)
-            packed[i:i + count, :, pl.ds(pl.multiple_of(c * 256, 256), 256)] = part_c
-
-        loop(places, body)
+            packed[i:i + count, :, c * 256:(c + 1) * 256] = part_c
 
     def pk_copy(i):
         return remote(packed.at[i], packed2.at[i], pk_send.at[i], pk_recv.at[i], across)
@@ -251,7 +267,6 @@
     def sb_copy(i):
         return remote(sb.at[i], sb2.at[i], sb_send.at[i], sb_recv.at[i], across)
 
-    build(valid, choose)
     pack(0, 2)
     pk_copy(0).start()
     pk_copy(1).start()
@@ -335,7 +350,7 @@
             other = source_matrix(*[f[g * GB:(g + 1) * GB] for f in far])
 
             def far_tile(o, m):
-                row = ((i + 1) % 2 * 2 + o) * PB + half * PAIR + g * GB
+                row = (i % 2 * 2 + o) * PB + half * PAIR + g * GB
                 return w2[m, pl.ds(pl.multiple_of(row, GB), GB), :]
 
             groups.append(jnp.dot(
@@ -347,20 +362,20 @@
             ))
         store_chunk(NY + k, groups)
 
-    def unpack(i, count):
-        for piece in range(count):
+    def unpack(i):
+        for piece in range(2):
             pk_copy(i + piece).wait_recv()
             sb_copy(i + piece).wait_recv()
-        rows = packed2[pl.ds(i, count)].reshape(count * 2 * PB, CAP)
-
-        def body(m):
-            lanes_m = pl.ds(pl.multiple_of(m * channels, channels), channels)
-            side = choose2[:, :, lanes_m].reshape(CAP, channels)
-            w2[m, (2 - count) * 2 * PB:4 * PB] = jnp.dot(
-                rows, side, preferred_element_type=jnp.float32
+        rows = packed2[pl.ds(i, 2)].reshape(4 * PB, CAP)
+
+        def body(m, count):
+            lanes_m = lane_block(m)
+            side = choose2[0:count, :, lanes_m].reshape(count * channels, channels)
+            w2[m] = jnp.dot(
+                rows[:, :count * channels], side, preferred_element_type=jnp.float32
             )
 
-        loop(m_count, body)
+        by_segment(body)
 
     def ring(n):
         def copy(i):
@@ -426,7 +441,7 @@
         def at(lag, body):
             pl.when((n >= lag) & (n < chunks + lag))(lambda: body(n - lag))
 
-        @pl.when(n == NY - 1)
+        @pl.when(n == NY // 2)
         def _():
             pack(2, PIECES - 2)
             for i in range(2, PIECES):
@@ -437,7 +452,7 @@
         at(LAG[1], ring_sum)
         at(LAG[2], ring_end)
 
-        @pl.when(n == NY)
+        @pl.when(n == NY - 2)
         def _():
             v_copy.wait_recv()
             build(valid2, choose2)
@@ -446,13 +461,9 @@
         def _():
             correlate_own(n)
 
-        @pl.when(n == NY)
-        def _():
-            unpack(0, 1)
-
-        @pl.when((n > NY) & (n < chunks) & ((n - NY) % 4 == 2))
-        def _():
-            unpack((n - NY) // 2, 2)
+        @pl.when((n >= NY) & (n < chunks) & ((n - NY) % 4 == 0))
+        def _():
+            unpack((n - NY) // 2)
 
         @pl.when((n >= NY) & (n < chunks))
         def _():

time: 90.1 us -> 82 us (0.910)
  Pallas kernels: 86.1 us -> 78 us
    pallas_call x1, Pallas kernels: 86.1 us -> 78 us  [on_device(): pl.pallas_call(functools.partial(kernel, (nb, nt, segments, length)), out...]
where the time goes in v5:
time: 82 us; the launch traced here: 81.8 us
  Pallas kernels  78 us (95%)
  matrix products  3.81 us (5%)
    pallas_call x1, Pallas kernels, on_device(): pl.pallas_call(functools.partial(kernel, (nb, nt, segments, length)), out...  78 us
    dot_general x1, matrix products, on_device(): lax.dot_general(cross, inverse, (((1,), (0,)), ((), ())), preferred_eleme...  3.81 us

profile of v5, /device:TPU:0, one launch (start us, length us, event | category | flops | bytes accessed | tf_op | source)
XLA Modules:
  0.0 81.8 jit_solution(4185070439812841460)
XLA Ops:
  0.0 0.0 copy-start
  0.0 78.0 %cross.1 = bf16[2,32,32,256]{3,2,1,0:T(8,128)(2,1)} custom-call(bf16[256,6,2,1024]{3,2,1,0:T(2,128)(2,1)} %bitcast.6, bf16[1024,1024]{1,0:T(8,128)(2,1)} %constant.4.clone.ft_hbm, s32[6,2,256]{2,1,0:T(2,128)} %bitcast.8, s32[4]{0:T(128)} %owner.1, s32[4]{0:T(128)} %first.1), custom_call_target="tpu_custom_call" | custom-call | tf_op jit(solution)/shard_map/cross/pallas_call | solution.py:521
  78.0 0.0 copy-done
  78.0 3.8 %fusion = f32[2,256,1024]{2,1,0:T(8,128)} fusion(bf16[2,1024,256]{2,1,0:T(8,128)(2,1)} %bitcast.7, bf16[1024,1024,1]{1,0,2:T(8,128)(2,1)S(1)} %copy-done), kind=kOutput, calls=%fused_computation | convolution fusion | flops 1073741824 | bytes 5242880 | tf_op jit(solution)/shard_map/dot_general | solution.py:564
Async XLA Ops:
  0.0 78.0 %copy-start = (bf16[1024,1024,1]{1,0,2:T(8,128)(2,1)S(1)}, bf16[1024,1024,1]{1,0,2:T(8,128)(2,1)}, u32[]{:S(2)}) copy-start(bf16[1024,1024,1]{1,0,2:T(8,128)(2,1)} %constant.8) | copy-start | bytes 6291460

commit v6 on v5

--- a/solution.py
+++ b/solution.py
@@ -201,7 +201,7 @@
         lax.fori_loop(low, high, step, 0)
 
     pltpu.make_async_copy(ft_hbm, ftv, ft_sem).wait()
-    transforms(0, 4)
+    transforms(0, 3)
 
     rsb[b] = slab[part, core]
     loop(nb, rs_arrived, b)
@@ -231,7 +231,7 @@
 
     loop(nr, lambda r: ag_copy(r).start(), part)
     fw_copy(part).start()
-    transforms(4, segments)
+    transforms(3, segments)
 
     def forward(r):
         arrived(r, core)

time: 82 us -> 81 us (0.988)
  Pallas kernels: 78 us -> 77.1 us
    pallas_call x1, Pallas kernels: 78 us -> 77.1 us  [on_device(): pl.pallas_call(functools.partial(kernel, (nb, nt, segments, length)), out...]
where the time goes in v6:
time: 81 us; the launch traced here: 80.9 us
  Pallas kernels  77.1 us (95%)
  matrix products  3.81 us (5%)
    pallas_call x1, Pallas kernels, on_device(): pl.pallas_call(functools.partial(kernel, (nb, nt, segments, length)), out...  77.1 us
    dot_general x1, matrix products, on_device(): lax.dot_general(cross, inverse, (((1,), (0,)), ((), ())), preferred_eleme...  3.81 us

profile of v6, /device:TPU:0, one launch (start us, length us, event | category | flops | bytes accessed | tf_op | source)
XLA Modules:
  0.0 80.9 jit_solution(14838450426946567619)
XLA Ops:
  0.0 0.0 copy-start
  0.0 77.1 %cross.1 = bf16[2,32,32,256]{3,2,1,0:T(8,128)(2,1)} custom-call(bf16[256,6,2,1024]{3,2,1,0:T(2,128)(2,1)} %bitcast.6, bf16[1024,1024]{1,0:T(8,128)(2,1)} %constant.4.clone.ft_hbm, s32[6,2,256]{2,1,0:T(2,128)} %bitcast.8, s32[4]{0:T(128)} %owner.1, s32[4]{0:T(128)} %first.1), custom_call_target="tpu_custom_call" | custom-call | tf_op jit(solution)/shard_map/cross/pallas_call | solution.py:521
  77.1 0.0 copy-done
  77.1 3.8 %fusion = f32[2,256,1024]{2,1,0:T(8,128)} fusion(bf16[2,1024,256]{2,1,0:T(8,128)(2,1)} %bitcast.7, bf16[1024,1024,1]{1,0,2:T(8,128)(2,1)S(1)} %copy-done), kind=kOutput, calls=%fused_computation | convolution fusion | flops 1073741824 | bytes 5242880 | tf_op jit(solution)/shard_map/dot_general | solution.py:564
Async XLA Ops:
  0.0 77.1 %copy-start = (bf16[1024,1024,1]{1,0,2:T(8,128)(2,1)S(1)}, bf16[1024,1024,1]{1,0,2:T(8,128)(2,1)}, u32[]{:S(2)}) copy-start(bf16[1024,1024,1]{1,0,2:T(8,128)(2,1)} %constant.8) | copy-start | bytes 6291460
